TPU v7x, 256 devices: a whole 4x4x8 slice. The times are simulated.
256 devices in a mesh: section: 2 (over z_lo), dp: 16 (over y, z_hi), tensor: 8 (over x, core).
Axes of the slice: x: 4, y: 4, z: 8 (z_hi: 4, z_lo: 2; z = z_hi * 2 + z_lo), core: 2. Of those that a mesh axis runs over, the one named last changes fastest.
Arguments:
- byte_rows: bfloat16 [2, 16, 512, 4672], P('section', 'dp', None, 'tensor'), may hold values from -1.75 to 1.75
- context: bfloat16 [2, 16, 512, 4096], P('section', 'dp', None, 'tensor'), may hold values from -1.75 to 1.75
- weight: bfloat16 [2, 4672, 4096], P('section', 'dp', 'tensor'), may hold values from -0.09375 to 0.09375
- keep_list: int32 [16, 512], P('dp'), may hold values from 0 to 511, as said below
- counts: int32 [16], P('dp'), may hold values from 128 to 512, as said below
- gate_vector: float32 [4672], P('tensor'), may hold values from -0.09375 to 0.09375
Outputs:
- section_rows: bfloat16 [2, 16, 512, 4672], P('section', 'dp', None, 'tensor')
- gate_values: bfloat16 [2, 16, 512], P('section', 'dp')
- context_grad: bfloat16 [2, 16, 512, 4096], P('section', 'dp', None, 'tensor')
- weight_grad: bfloat16 [2, 4672, 4096], P('section', 'dp', 'tensor')
Inputs may be any that keep to these rules, and one draw needn't show every extreme that they name: `keep_list`: for each sequence b, entries 0 to counts[b] - 1 are distinct byte positions in increasing order; the entries after them are 0. `counts`: some sequence keeps all 512 bytes.
All inputs are finite; a program needn't handle non-finite values.
Results may differ from a plain program's by a relative error of at most 0.02.
Values may be sent and summed in bfloat16 or wider, within the bound.
A program may use at most 64 MiB of HBM per device.

v0:
```python
import jax
import jax.numpy as jnp
from jax import lax
from jax.sharding import PartitionSpec as P

D = 4672


epsilon = 1e-06
sharpness = 30.0


def partner(block, axis, bit):
    count = lax.axis_size(axis)
    route = []
    for low in range(count):
        high = low | 1 << bit
        if high != low and high < count:
            route += [(low, high), (high, low)]
    return lax.ppermute(block, axis, route)


def pick_rows(table, index):
    return table[index]


def spread_rows(index, values):
    return jnp.zeros(values.shape, jnp.float32).at[index].add(values)


def per_device(byte_rows, context, weight, keep_list, counts, gate_vector):
    section_index = lax.axis_index("section")
    is_early = section_index == 0
    residual = byte_rows[0]
    context_rows = context[0]
    live_rows = lax.broadcasted_iota(jnp.int32, residual.shape[:2], 1) < counts[:, None]
    live_wide = live_rows[:, :, None]
    full_weight = lax.all_gather(weight[0], "dp", axis=0, tiled=True)
    projected_part = jnp.einsum(
        "bpi,di->bpd", context_rows, full_weight, preferred_element_type=jnp.float32
    )
    projected = lax.psum_scatter(
        projected_part.astype(jnp.bfloat16), "tensor", scatter_dimension=2, tiled=True
    ).astype(jnp.float32)
    early_out = (residual.astype(jnp.float32) + projected).astype(jnp.bfloat16)
    hidden_wide = early_out.astype(jnp.float32)
    square_sum, gate_dot = lax.psum(
        (jnp.sum(hidden_wide * hidden_wide, axis=-1), jnp.sum(hidden_wide * gate_vector, axis=-1)),
        "tensor",
    )
    inverse_rms = lax.rsqrt(square_sum / D + epsilon)
    gate_score = inverse_rms * gate_dot
    squashed = jax.nn.sigmoid(gate_score)
    gate_value = (-sharpness * squashed).astype(jnp.bfloat16)
    packed = jax.vmap(pick_rows)(early_out, keep_list)
    packed = jnp.where(live_wide, packed, jnp.zeros_like(packed))
    packed_gate = jnp.where(
        live_rows, jax.vmap(pick_rows)(gate_value, keep_list), jnp.zeros_like(gate_value)
    )
    outgoing = jnp.where(is_early, packed, residual)
    arrived, arrived_gate = partner((outgoing, packed_gate), "section", 0)
    returned_grad = jnp.where(live_wide, arrived, jnp.zeros_like(arrived))
    spread = jax.vmap(spread_rows)(keep_list, returned_grad.astype(jnp.float32))
    score_grad = -sharpness * squashed * (1.0 - squashed)
    gate_part = score_grad[:, :, None] * (
        inverse_rms[:, :, None] * gate_vector
        - (gate_score * inverse_rms * inverse_rms / D)[:, :, None] * hidden_wide
    )
    early_grad = (spread + gate_part).astype(jnp.bfloat16)
    late_out = jnp.where(live_wide, arrived.astype(jnp.float32) + projected, 0.0).astype(
        jnp.bfloat16
    )
    late_grad = jnp.where(live_wide, residual, jnp.zeros_like(residual))
    grad_rows = jnp.where(is_early, early_grad, late_grad)
    section_rows = jnp.where(is_early, early_grad, late_out)[None]
    gate_values = jnp.where(is_early, gate_value, arrived_gate)[None]
    gathered = lax.all_gather(grad_rows, "tensor", axis=2, tiled=True)
    ctx_total = jnp.einsum("bpd,di->bpi", gathered, full_weight, preferred_element_type=jnp.float32)
    weight_share = lax.psum_scatter(
        jnp.einsum(
            "bpd,bpi->di", gathered, context_rows, preferred_element_type=jnp.float32
        ).astype(jnp.bfloat16),
        "dp",
        scatter_dimension=0,
        tiled=True,
    )
    context_grad = ctx_total.astype(jnp.bfloat16)[None]
    weight_grad = weight_share[None]
    return (section_rows, gate_values, context_grad, weight_grad)


def solution(mesh):
    placed = (
        P("section", "dp", None, "tensor"),
        P("section", "dp", None, "tensor"),
        P("section", "dp", "tensor"),
        P("dp", None),
        P("dp"),
        P("tensor"),
    )
    return jax.shard_map(
        per_device,
        mesh=mesh,
        in_specs=placed,
        out_specs=(
            P("section", "dp", None, "tensor"),
            P("section", "dp", None),
            P("section", "dp", None, "tensor"),
            P("section", "dp", "tensor"),
        ),
        check_vma=False,
    )
```

profile of v0, /device:TPU:19, one launch (start us, length us, event | category | flops | bytes accessed | tf_op | source)
XLA Modules:
  0.0 413.7 jit_solution(7643077002853015245)
XLA Ops:
  7.2 0.0 copy-start
  7.2 0.0 all-gather.6.cloned.1.call-start
  7.2 2.3 copy.23
  9.5 0.0 all-gather.6.cloned.1.call-update
  9.5 0.0 reduce-scatter.4.cloned.1.call-start
  9.6 124.2 %all-gather.6.cloned.1.call-done = bf16[1,4672,512]{2,0,1:T(2,128)(2,1)} async-done(((bf16[1,292,512]{2,0,1:T(2,128)(2,1)}), bf16[1,4672,512]{2,0,1:T(2,128)(2,1)}) %all-gather.6.cloned.1.call-update) | async-done | bytes 4784144 | tf_op jit(solution)/shard_map/all_gather | solution.py:38
  133.8 0.0 copy-done
  133.8 8.1 %fusion.1 = bf16[1,512,4672]{1,2,0:T(8,128)(2,1)} fusion(bf16[1,4672,512]{2,0,1:T(2,128)(2,1)} %all-gather.6.cloned.1.call-done, bf16[1,1,512,512]{3,2,1,0:T(8,128)(2,1)S(1)} %copy-done), kind=kOutput, calls=%fused_computation.5 | convolution fusion | flops 2451865600 | bytes 10092544 | tf_op jit(solution)/shard_map/bpi,di->bpd/dot_general | solution.py:39
  141.9 0.0 copy-start.5
  141.9 0.0 copy-start.1
  141.9 0.0 copy-start.4
  141.9 0.0 reduce-scatter.4.cloned.1.call-update
  142.0 0.0 all-gather.4.cloned.1.call-start
  142.7 0.0 copy-done.5
  142.8 44.6 %reduce-scatter.4.cloned.1.call-done = bf16[1,512,584]{1,2,0:T(8,128)(2,1)} async-done(((bf16[1,512,4672]{1,2,0:T(8,128)(2,1)}), bf16[1,512,584]{1,2,0:T(8,128)(2,1)}) %reduce-scatter.4.cloned.1.call-update) | async-done | bytes 598032 | tf_op jit(solution)/shard_map/reduce_scatter | solution.py:42
  187.4 0.0 copy-done.1
  187.4 0.0 copy-done.4
  187.4 1.4 fusion.22
  188.8 0.3 copy.24
  189.1 3.5 gather_fusion
  192.6 0.2 copy.25
  192.9 0.9 fusion.29
  193.8 1.5 collective-permute-start
  195.3 13.1 %all-reduce.2 = (f32[1,512]{1,0:T(1,128)S(1)}, f32[1,512]{1,0:T(1,128)S(1)}) all-reduce(f32[1,512]{1,0:T(1,128)S(1)} %bitcast.72, f32[1,512]{1,0:T(1,128)S(1)} %bitcast.71), channel_id=1, replica_groups=mesh['section'=2,'dp'=16,'tensor'=8] {'tensor'}, use_global_device_ids=true, to_apply=%region_4.0 | all-reduce | flops 1024 | bytes 8192 | tf_op jit(solution)/shard_map/psum | solution.py:47
  208.4 1.3 fusion.26
  209.7 1.7 copy.26
  211.4 0.0 collective-permute-done
  211.4 0.0 copy-start.3
  211.4 1.2 bitcast_convert_fusion
  212.6 2.8 copy.27
  215.4 0.0 copy-done.3
  215.4 5.2 %scatter_fusion = f32[512,584]{1,0:T(8,128)S(1)} fusion(f32[512,584]{1,0:T(8,128)S(1)} %copy.26, s32[512]{0:T(512)S(1)} %bitcast.73, f32[512,584]{1,0:T(8,128)} %copy.27), kind=kCustom, calls=%fused_computation.2 | custom fusion | flops 299008 | bytes 3590144 | tf_op jit(solution)/shard_map/vmap()/scatter-add | solution.py:28
  220.5 0.0 copy-start.2
  220.6 1.0 copy.28
  221.6 0.0 copy-done.2
  221.6 2.7 bitcast_select_fusion
  224.3 0.0 copy-start.6
  224.3 0.0 all-gather.4.cloned.1.call-update
  224.3 3.5 gather_fusion.1
  227.8 0.1 collective-permute-start.1
  227.9 0.0 copy-done.6
  227.9 0.6 dynamic-slice.4
  229.2 1.1 collective-permute-done.1
  230.3 0.6 fusion.33
  230.9 31.4 %all-gather.4.cloned.1.call-done = bf16[1,512,4672]{1,2,0:T(8,128)(2,1)} async-done(((bf16[1,512,584]{1,2,0:T(8,128)(2,1)}), bf16[1,512,4672]{1,2,0:T(8,128)(2,1)}) %all-gather.4.cloned.1.call-update) | async-done | bytes 4784144 | tf_op jit(solution)/shard_map/all_gather | solution.py:77
  262.3 6.7 %convolution_convert_fusion = bf16[4672,512]{1,0:T(8,128)(2,1)} fusion(bf16[1,512,4672]{1,2,0:T(8,128)(2,1)} %all-gather.4.cloned.1.call-done, bf16[1,1,512,512]{3,2,1,0:T(8,128)(2,1)S(1)} %copy-done), kind=kOutput, calls=%fused_computation.3 | convolution fusion | flops 2451865600 | bytes 10092544 | tf_op jit(solution)/shard_map/bpd,bpi->di/dot_general | solution.py:80
  269.0 123.1 %fusion = bf16[296,512]{1,0:T(8,128)(2,1)S(1)} fusion(bf16[4672,512]{1,0:T(8,128)(2,1)} %convolution_convert_fusion), kind=kCustom, calls=%all-reduce-scatter | all-reduce-scatter fusion | flops 2424833 | bytes 5088256
  392.1 5.0 %collective-permute-start.2 = (bf16[60,512]{1,0:T(8,128)(2,1)S(1)}, bf16[60,512]{1,0:T(8,128)(2,1)S(1)}, u32[]{:S(2)}, u32[]{:S(2)}) collective-permute-start(bf16[60,512]{1,0:T(8,128)(2,1)S(1)} %slice.8), channel_id=1, source_target_pairs={{0,8},{8,16},{16,24},{24,32},{32,40},{40,48},{48,56},{56,64},{64,7... | collective-permute-start | bytes 184328
  397.1 8.7 %fusion.14 = bf16[1,1,512,512]{3,2,1,0:T(8,128)(2,1)} fusion(bf16[1,4672,512]{2,0,1:T(2,128)(2,1)} %all-gather.6.cloned.1.call-done, bf16[1,512,4672]{1,2,0:T(8,128)(2,1)} %all-gather.4.cloned.1.call-done), kind=kOutput, calls=%fused_computation.19 | convolution fusion | flops 2449735680 | bytes 10092544 | tf_op jit(solution)/shard_map/bpd,di->bpi/dot_general | solution.py:78
  405.8 0.0 collective-permute-done.2
  405.8 0.5 concatenate.8
  406.4 0.8 dynamic-slice_bitcast_fusion
  (8 shorter events, 0.1 us)
Async XLA Ops:
  7.2 126.6 %copy-start = (bf16[1,1,512,512]{3,2,1,0:T(8,128)(2,1)S(1)}, bf16[1,1,512,512]{3,2,1,0:T(8,128)(2,1)}, u32[]{:S(2)}) copy-start(bf16[1,1,512,512]{3,2,1,0:T(8,128)(2,1)} %param.7) | copy-start | bytes 1572868
  7.2 126.6 %all-gather.6.cloned.1.call-start = ((), (), s32[]{:S(2)}) async-start(), calls=%async_computation.3 | async-start | bytes 10166272 | tf_op jit(solution)/shard_map/all_gather | solution.py:38
  9.5 177.9 %reduce-scatter.4.cloned.1.call-start = ((), (), s32[]{:S(2)}) async-start(), calls=%async_computation.1 | async-start | bytes 5382144 | tf_op jit(solution)/shard_map/reduce_scatter | solution.py:42
  141.9 0.8 copy-start.5
  141.9 45.5 %copy-start.1 = (bf16[1,1,512,584]{2,3,1,0:T(8,128)(2,1)S(1)}, bf16[1,1,512,584]{2,3,1,0:T(8,128)(2,1)}, u32[]{:S(2)}) copy-start(bf16[1,1,512,584]{2,3,1,0:T(8,128)(2,1)} %param.6) | copy-start | bytes 1794052
  141.9 45.5 %copy-start.4 = (f32[584]{0:T(1024)S(1)}, f32[584]{0:T(1024)}, u32[]{:S(2)}) copy-start(f32[584]{0:T(1024)} %param.11) | copy-start | bytes 7012
  142.0 120.3 %all-gather.4.cloned.1.call-start = ((), (), s32[]{:S(2)}) async-start(), calls=%async_computation.2 | async-start | bytes 5382144 | tf_op jit(solution)/shard_map/all_gather | solution.py:77
  193.8 17.6 %collective-permute-start = (bf16[1,512,584]{1,2,0:T(8,128)(2,1)}, bf16[1,512,584]{1,2,0:T(8,128)(2,1)S(1)}, u32[]{:S(2)}, u32[]{:S(2)}) collective-permute-start(bf16[1,512,584]{1,2,0:T(8,128)(2,1)} %fusion.29), channel_id=1, source_target_pairs={{0,128},{128,0},{1,129},{129,1},{2,130},{130,2},{3,131},{131,3},{4... | collective-permute-start | bytes 1794056 | tf_op jit(solution)/shard_map/ppermute | solution.py:20
  211.4 4.0 copy-start.3
  220.5 1.1 copy-start.2
  224.3 3.7 copy-start.6
  227.8 2.5 collective-permute-start.1
  392.1 13.7 %collective-permute-start.2 = (bf16[60,512]{1,0:T(8,128)(2,1)S(1)}, bf16[60,512]{1,0:T(8,128)(2,1)S(1)}, u32[]{:S(2)}, u32[]{:S(2)}) collective-permute-start(bf16[60,512]{1,0:T(8,128)(2,1)S(1)} %slice.8), channel_id=1, source_target_pairs={{0,8},{8,16},{16,24},{24,32},{32,40},{40,48},{48,56},{56,64},{64,7... | collective-permute-start | bytes 184328
Sparse Core Ops, SparseCore 0:
  11.1 122.6 all-gather.5
  142.1 45.2 reduce-scatter.3
  224.4 37.8 all-gather.3
where the time goes:
time: 417 us; the launch traced here: 414 us
  waiting for transfers between devices  201 us (48%)
  blocking collectives  136 us (33%)
  matrix products  23.6 us (6%)
  local copies, waits for them, and re-layouts  17.3 us (4%)
  between operations  15.3 us (4%)
  other arithmetic  13.2 us (3%)
  starting transfers between devices  6.73 us (2%)
    all_gather x1, waiting for transfers between devices, per_device(): full_weight = lax.all_gather(weight[0], 'dp', axis=0, tiled=True)  124 us
    unnamed x1, blocking collectives  123 us
    reduce_scatter x1, waiting for transfers between devices, per_device(): lax.psum_scatter(projected_part.astype(jnp.bfloat16), 'tensor', scatter_d...  44.6 us
    all_gather x1, waiting for transfers between devices, per_device(): gathered = lax.all_gather(grad_rows, 'tensor', axis=2, tiled=True)  31.4 us
    psum x1, blocking collectives, per_device(): lax.psum((jnp.sum(hidden_wide * hidden_wide, axis=-1), jnp.sum(hidden_wid...  13.1 us
    dot_general x1, matrix products, per_device(): jnp.einsum('bpd,di->bpi', gathered, full_weight, preferred_element_type=j...  8.73 us
  transfers between devices with their start and end apart: 6, of which 4 were waited for; matrix products, arithmetic and copies ran while one was open for 4% of the time, Pallas kernels for 0%

commit v1 on v0

v1 whole, which is shorter than its diff:
```python
import jax
import jax.numpy as jnp
from jax import lax
from jax.experimental import pallas as pl
from jax.experimental.pallas import tpu as pltpu
from jax.sharding import PartitionSpec as P

D = 4672
SLAB = 292
PAD = 304
HEAD = 160
TAIL = PAD - HEAD
LEN = 512
INNER_DEV = 512
EPSILON = 1e-06
SHARPNESS = 30.0

MESH = pl.DeviceIdType.MESH
F32 = jnp.float32
BF16 = jnp.bfloat16


def place():
    s = lax.axis_index("section")
    d = lax.axis_index("dp")
    t = lax.axis_index("tensor")
    return s, lax.div(d, 4), lax.rem(d, 4), lax.div(t, 2), lax.rem(t, 2)


def device(s, y, z, x, c):
    return (s, y * 4 + z, x * 2 + c)


def turn(i, step):
    return lax.rem(i + step, 4)


def send(src, dst, send_sem, recv_sem, to):
    return pltpu.make_async_remote_copy(
        src_ref=src,
        dst_ref=dst,
        send_sem=send_sem,
        recv_sem=recv_sem,
        device_id=to,
        device_id_type=MESH,
    )


def greet(peers):
    barrier = pltpu.get_barrier_semaphore()
    for peer in peers:
        pl.semaphore_signal(barrier, inc=1, device_id=peer, device_id_type=MESH)
    pl.semaphore_wait(barrier, len(peers))


def forward_kernel(
    w_ref, ctx_ref, byte_ref, g_ref, kcol_ref, krow_ref,
    grad_ref, e_ref, proj_ref, gate_ref, wout_ref,
    wf, part, ra, rb, xin, spread, st_out, st_in,
    ws, wr, as_, ar, bs, br, xs, ss, sr, ls,
):
    s, y, z, x, c = place()
    t = x * 2 + c
    up, down = device(s, turn(y, 1), z, x, c), device(s, turn(y, 3), z, x, c)
    right, left = device(s, y, turn(z, 1), x, c), device(s, y, turn(z, 3), x, c)
    sibling = device(s, y, z, x, 1 - c)
    partner = device(1 - s, y, z, x, c)
    team = [(s, y * 4 + z, lax.rem(t + j, 8)) for j in range(1, 8)]
    greet([up, down, right, left, partner] + team)

    started = []

    def go(copy):
        copy.start()
        started.append(copy)

    def slab(yy, zz):
        return yy * 4 + zz

    def whole(ref, k):
        return ref.at[k]

    def head(ref, k):
        return ref.at[k, pl.ds(0, HEAD)]

    def tail(ref, k):
        return ref.at[k, pl.ds(HEAD, TAIL)]

    def arrived(k):
        send(wf.at[k], wf.at[k], ws.at[0], wr.at[k, 0], up).wait_recv()

    def arrived_halves(k):
        send(head(wf, k), head(wf, k), ws.at[0], wr.at[k, 0], up).wait_recv()
        send(tail(wf, k), tail(wf, k), ws.at[0], wr.at[k, 1], up).wait_recv()

    own = slab(y, z)

    go(send(w_ref, wf.at[own], ws.at[4], wr.at[own, 0], up))
    go(send(w_ref, wf.at[own], ws.at[5], wr.at[own, 0], down))
    go(send(w_ref, wf.at[own], ws.at[0], wr.at[own, 0], right))
    go(send(w_ref, wf.at[own], ws.at[1], wr.at[own, 0], left))

    rows_out = send(byte_ref, xin, xs.at[0], xs.at[1], partner)

    @pl.when(s == 1)
    def _():
        rows_out.start()

    wf[own] = w_ref[...]

    def y_whole(zz, g):
        k = slab(y, zz)
        go(send(wf.at[k], wf.at[k], ws.at[4 + 4 * g], wr.at[k, 0], up))
        go(send(wf.at[k], wf.at[k], ws.at[5 + 4 * g], wr.at[k, 0], down))

    def y_halves(zz, g):
        below, above = slab(turn(y, 3), zz), slab(turn(y, 1), zz)
        arrived(below)
        go(send(head(wf, below), head(wf, below), ws.at[6 + 4 * g], wr.at[below, 0], up))
        arrived(above)
        go(send(tail(wf, above), tail(wf, above), ws.at[7 + 4 * g], wr.at[above, 1], down))

    def slot(yy, zz):
        return yy * 2 + lax.rem(zz, 2)

    def mine(zz):
        return lax.div(zz, 2) == c

    def to_sibling(yy, zz):
        i = slot(yy, zz)
        return send(part.at[slab(yy, zz)], ra.at[i], as_.at[i], ar.at[i], sibling)

    def to_owner(yy, zz):
        i, j = slot(yy, zz), x * 2 + lax.rem(zz, 2)
        return send(
            part.at[slab(yy, zz)], rb.at[j], bs.at[i], br.at[j], device(s, y, z, yy, c)
        )

    def project(yy, zz):
        k = slab(yy, zz)
        part[k] = lax.dot_general(
            wf[k], ctx_ref[...], (((1,), (1,)), ((), ())), preferred_element_type=F32
        ).astype(BF16)

        @pl.when(jnp.logical_not(mine(zz)))
        def _():
            to_sibling(yy, zz).start()

    def collect(yy, zz):
        @pl.when(mine(zz))
        def _():
            k = slab(yy, zz)
            to_sibling(yy, zz).wait_recv()
            part[k] = (part[k].astype(F32) + ra[slot(yy, zz)].astype(F32)).astype(BF16)

            @pl.when(yy != x)
            def _():
                to_owner(yy, zz).start()

    def work(count, pick):
        if count == 1:
            project(*pick(0))
            collect(*pick(0))
            return

        @pl.loop(0, count)
        def _(i):
            project(*pick(i))

        @pl.loop(0, count)
        def _(i):
            collect(*pick(i))

    z2 = turn(z, 2)
    y2 = turn(y, 2)

    def beside(zz):
        return lambda i: (turn(y, 1 + 2 * i), zz)

    work(1, lambda i: (y, z))
    y_halves(z, 0)
    work(2, beside(z))
    arrived_halves(slab(y2, z))
    work(1, lambda i: (y2, z))

    zr, zl = turn(z, 1), turn(z, 3)
    arrived(slab(y, zl))
    go(send(head(wf, slab(y, zl)), head(wf, slab(y, zl)), ws.at[2], wr.at[slab(y, zl), 0], right))
    y_whole(zl, 1)
    arrived(slab(y, zr))
    go(send(tail(wf, slab(y, zr)), tail(wf, slab(y, zr)), ws.at[3], wr.at[slab(y, zr), 1], left))
    y_whole(zr, 2)
    work(2, lambda i: (y, turn(z, 3 - 2 * i)))

    place_of = lax.broadcasted_iota(jnp.int32, (LEN, LEN), 1)

    @pl.when(s == 0)
    def _():
        rows_out.wait_recv()
        pick = jnp.where(kcol_ref[...] == place_of, 1.0, 0.0).astype(BF16)
        for i in range(2):
            spread[i] = jnp.dot(xin[i], pick, preferred_element_type=F32).astype(BF16)

    y_halves(zl, 1)
    arrived_halves(slab(y, z2))
    y_whole(z2, 3)
    work(2, beside(zl))
    work(1, lambda i: (y, z2))
    y_halves(zr, 2)
    work(2, beside(zr))
    arrived_halves(slab(y2, zl))
    arrived_halves(slab(y2, zr))
    work(2, lambda i: (y2, turn(z, 3 - 2 * i)))
    y_halves(z2, 3)
    work(2, beside(z2))
    arrived_halves(slab(y2, z2))
    keep_weight = pltpu.make_async_copy(wf, wout_ref, ls.at[0])
    keep_weight.start()
    work(1, lambda i: (y2, z2))

    def total_of(i):
        total = part[t * 2 + i].astype(F32)
        for step in range(1, 4):
            j = turn(x, step) * 2 + i
            send(rb.at[j], rb.at[j], bs.at[0], br.at[j], up).wait_recv()
            total = total + rb[j].astype(F32)
        return total

    @pl.when(s == 0)
    def _():
        st_out[...] = jnp.zeros_like(st_out)
        for i in range(2):
            e = (byte_ref[i].astype(F32) + total_of(i)).astype(BF16)
            e_ref[i] = e
            e = e.astype(F32)
            st_out[0:1] += jnp.sum(e * e, axis=0, keepdims=True)
            st_out[1:2] += jnp.sum(e * g_ref[i], axis=0, keepdims=True)
        st_in[t] = st_out[...]
        stats = [
            send(st_out, st_in.at[t], ss.at[j], sr.at[j], peer) for j, peer in enumerate(team)
        ]
        for copy in stats:
            copy.start()
        for copy in stats:
            copy.wait()
        sums = st_in[0]
        for j in range(1, 8):
            sums = sums + st_in[j]
        inverse = lax.rsqrt(sums[0:1] / D + EPSILON)
        score = inverse * sums[1:2]
        squashed = jax.nn.sigmoid(score)
        gate = (-SHARPNESS * squashed).astype(BF16)
        gate_ref[...] = jnp.broadcast_to(gate, gate_ref.shape)
        slope = -SHARPNESS * squashed * (1.0 - squashed)
        pull = score * inverse * inverse / D
        for i in range(2):
            gate_part = slope * (inverse * g_ref[i] - pull * e_ref[i].astype(F32))
            grad_ref[i] = (spread[i].astype(F32) + gate_part).astype(BF16)

    @pl.when(s == 1)
    def _():
        live = krow_ref[...] >= 0
        for i in range(2):
            proj_ref[i] = total_of(i)
            rows = byte_ref[i]
            grad_ref[i] = jnp.where(live, rows, jnp.zeros_like(rows))
        rows_out.wait_send()

    for copy in started:
        copy.wait_send()

    @pl.loop(0, 16)
    def _(k):
        yy, zz = lax.div(k, 4), lax.rem(k, 4)

        @pl.when(jnp.logical_not(mine(zz)))
        def _():
            to_sibling(yy, zz).wait_send()

        @pl.when(jnp.logical_and(mine(zz), yy != x))
        def _():
            to_owner(yy, zz).wait_send()

    keep_weight.wait()


def backward_kernel(
    grad_ref, e_ref, proj_ref, gate_ref, w_ref, ctx_ref, krow_ref,
    rows_ref, gout_ref, cgrad_ref, wgrad_ref,
    gf, wf, wp, yh, yr, ysum, zh, zr, xin, gin, cacc, last,
    gs, gr, hs, hr, fs, fr, zs, zrs, xs, ls,
):
    s, y, z, x, c = place()
    t = x * 2 + c
    up, down = device(s, turn(y, 1), z, x, c), device(s, turn(y, 3), z, x, c)
    right, left = device(s, y, turn(z, 1), x, c), device(s, y, turn(z, 3), x, c)
    east, west = device(s, y, z, turn(x, 1), c), device(s, y, z, turn(x, 3), c)
    sibling = device(s, y, z, x, 1 - c)
    partner = device(1 - s, y, z, x, c)
    load = pltpu.make_async_copy(w_ref, wf, ls.at[0])
    load.start()
    greet([up, down, right, left, east, west, sibling, partner])

    started = []

    def go(copy):
        copy.start()
        started.append(copy)

    def pass_on(k, i, to):
        go(send(gf.at[k], gf.at[k], gs.at[i], gr.at[k], to))

    def arrived(k):
        send(gf.at[k], gf.at[k], gs.at[0], gr.at[k], east).wait_recv()

    for i in range(2):
        k = t * 2 + i
        go(send(grad_ref.at[i], gf.at[k], gs.at[i], gr.at[k], east))
        go(send(grad_ref.at[i], gf.at[k], gs.at[2 + i], gr.at[k], west))
        go(send(grad_ref.at[i], gf.at[k], gs.at[4 + i], gr.at[k], sibling))
        gf[k] = grad_ref[i]

    rows_out = send(e_ref, xin, xs.at[0], xs.at[1], partner)
    gate_out = send(gate_ref, gin, xs.at[2], xs.at[3], partner)

    @pl.when(s == 0)
    def _():
        rows_out.start()
        gate_out.start()

    def halves(yy, zz):
        k = yy * 4 + zz
        return (
            send(wp.at[k, pl.ds(0, HEAD)], yh.at[0, zz], hs.at[0, zz], hr.at[0, zz], up),
            send(
                wp.at[k, pl.ds(HEAD, TAIL)], yh.at[1, zz, pl.ds(0, TAIL)],
                hs.at[1, zz], hr.at[1, zz], down,
            ),
        )

    def one_way(yy, zz, way, to):
        return send(wp.at[yy * 4 + zz], yr.at[way, zz], fs.at[way, zz], fr.at[way, zz], to)

    order = (2, 1, 3, 0)

    def compute(step):
        yy = turn(x, step)
        far = lax.rem(yy - y + 4, 4) == 2

        @pl.loop(0, 4)
        def _(i):
            zz = turn(z, i)
            k = yy * 4 + zz

            @pl.when(jnp.logical_and(lax.div(zz, 2) != c, True))
            def _():
                arrived(k)

            wp[k] = jnp.dot(gf[k], ctx_ref[...], preferred_element_type=F32).astype(BF16)

            @pl.when(far)
            def _():
                for copy in halves(yy, zz):
                    copy.start()

    def forward(step):
        yy = turn(x, step)
        rel = lax.rem(yy - y + 4, 4)
        for off in order:
            zz = turn(z, off)
            k = yy * 4 + zz
            to_head, to_tail = halves(yy, zz)

            @pl.when(rel == 1)
            def _():
                to_head.wait_recv()
                rows = pl.ds(0, HEAD)
                wp[k, rows] = (wp[k, rows].astype(F32) + yh[0, zz].astype(F32)).astype(BF16)
                one_way(yy, zz, 0, up).start()

            @pl.when(rel == 3)
            def _():
                to_tail.wait_recv()
                rows = pl.ds(HEAD, TAIL)
                wp[k, rows] = (
                    wp[k, rows].astype(F32) + yh[1, zz, pl.ds(0, TAIL)].astype(F32)
                ).astype(BF16)
                one_way(yy, zz, 1, down).start()

    def context_part(step):
        yy = turn(x, step)

        @pl.loop(0, 4)
        def _(i):
            k = yy * 4 + i
            cacc[...] += lax.dot_general(
                gf[k], wf[k], (((0,), (0,)), ((), ())), preferred_element_type=F32
            )

    cacc[...] = jnp.zeros_like(cacc)
    compute(0)
    xe, xw, xo = turn(x, 1), turn(x, 3), turn(x, 2)

    def from_west(i):
        k = (xw * 2 + c) * 2 + i
        arrived(k)
        if i == 0:
            pass_on(k, 6, east)
        pass_on(k, 8 + i, sibling)

    def from_east(i):
        k = (xe * 2 + c) * 2 + i
        arrived(k)
        if i == 1:
            pass_on(k, 7, west)
        pass_on(k, 10 + i, sibling)

    load.wait()
    context_part(0)
    from_west(0)
    from_east(0)
    from_west(1)
    from_east(1)
    forward(0)
    compute(1)
    compute(3)
    for i in range(2):
        k = (xo * 2 + c) * 2 + i
        arrived(k)
        pass_on(k, 12 + i, sibling)
    compute(2)
    context_part(1)
    forward(1)
    context_part(3)
    forward(3)
    forward(2)
    context_part(2)
    cgrad_ref[...] = cacc[...].astype(BF16)

    for off in order:
        zz = turn(z, off)
        k = y * 4 + zz
        one_way(y, zz, 0, up).wait_recv()
        one_way(y, zz, 1, down).wait_recv()
        total = wp[k].astype(F32) + yr[0, zz].astype(F32) + yr[1, zz].astype(F32)
        if off == 2:
            ysum[0] = total.astype(BF16)
            go(send(ysum.at[0, pl.ds(0, HEAD)], zh.at[0], zs.at[0], zrs.at[0], right))
            go(
                send(
                    ysum.at[0, pl.ds(HEAD, TAIL)], zh.at[1, pl.ds(0, TAIL)],
                    zs.at[1], zrs.at[1], left,
                )
            )
        elif off == 1:
            started[-2].wait_recv()
            ysum[1] = total.astype(BF16)
            rows = pl.ds(0, HEAD)
            ysum[1, rows] = (total[:HEAD] + zh[0].astype(F32)).astype(BF16)
            go(send(ysum.at[1], zr.at[0], zs.at[2], zrs.at[2], right))
        elif off == 3:
            started[-2].wait_recv()
            ysum[2] = total.astype(BF16)
            rows = pl.ds(HEAD, TAIL)
            ysum[2, rows] = (total[HEAD:] + zh[1, pl.ds(0, TAIL)].astype(F32)).astype(BF16)
            go(send(ysum.at[2], zr.at[1], zs.at[3], zrs.at[3], left))
        else:
            last[...] = total

    started[-2].wait_recv()
    started[-1].wait_recv()
    wgrad_ref[...] = (last[...] + zr[0].astype(F32) + zr[1].astype(F32)).astype(BF16)

    @pl.when(s == 0)
    def _():
        rows_ref[...] = grad_ref[...]
        gout_ref[...] = gate_ref[...]
        rows_out.wait_send()
        gate_out.wait_send()

    @pl.when(s == 1)
    def _():
        rows_out.wait_recv()
        gate_out.wait_recv()
        live = krow_ref[...] >= 0
        place_of = lax.broadcasted_iota(jnp.int32, (LEN, LEN), 0)
        pick = jnp.where(krow_ref[...] == place_of, 1.0, 0.0).astype(BF16)
        for i in range(2):
            packed = jnp.dot(xin[i], pick, preferred_element_type=F32)
            rows_ref[i] = jnp.where(live, packed + proj_ref[i], 0.0).astype(BF16)
        gout_ref[...] = jnp.dot(gin[...], pick, preferred_element_type=F32).astype(BF16)

    for copy in started:
        copy.wait_send()

    @pl.loop(0, 4)
    def _(zz):
        for copy in halves(turn(y, 2), zz):
            copy.wait_send()
        one_way(turn(y, 1), zz, 0, up).wait_send()
        one_way(turn(y, 3), zz, 1, down).wait_send()


VMEM = pl.BlockSpec(memory_space=pltpu.VMEM)
ANY = pl.BlockSpec(memory_space=pl.ANY)
LIMIT = 56 * 2**20


def forward_call(*operands):
    dma = pltpu.SemaphoreType.DMA
    return pl.pallas_call(
        forward_kernel,
        name="forward",
        out_shape=(
            jax.ShapeDtypeStruct((2, PAD, LEN), BF16),
            jax.ShapeDtypeStruct((2, PAD, LEN), BF16),
            jax.ShapeDtypeStruct((2, PAD, LEN), F32),
            jax.ShapeDtypeStruct((16, LEN), BF16),
            jax.ShapeDtypeStruct((16, PAD, INNER_DEV), BF16),
        ),
        in_specs=[VMEM] * 6,
        out_specs=(VMEM, VMEM, VMEM, VMEM, ANY),
        scratch_shapes=[
            pltpu.VMEM((16, PAD, INNER_DEV), BF16),
            pltpu.VMEM((16, PAD, LEN), BF16),
            pltpu.VMEM((8, PAD, LEN), BF16),
            pltpu.VMEM((8, PAD, LEN), BF16),
            pltpu.VMEM((2, PAD, LEN), BF16),
            pltpu.VMEM((2, PAD, LEN), BF16),
            pltpu.VMEM((8, LEN), F32),
            pltpu.VMEM((8, 8, LEN), F32),
            dma((20,)), dma((16, 2)), dma((8,)), dma((8,)), dma((8,)), dma((8,)),
            dma((2,)), dma((7,)), dma((7,)), dma((1,)),
        ],
        compiler_params=pltpu.CompilerParams(
            collective_id=0, has_side_effects=True, vmem_limit_bytes=LIMIT
        ),
    )(*operands)


def backward_call(*operands):
    dma = pltpu.SemaphoreType.DMA
    return pl.pallas_call(
        backward_kernel,
        name="backward",
        out_shape=(
            jax.ShapeDtypeStruct((2, PAD, LEN), BF16),
            jax.ShapeDtypeStruct((16, LEN), BF16),
            jax.ShapeDtypeStruct((LEN, INNER_DEV), BF16),
            jax.ShapeDtypeStruct((PAD, INNER_DEV), BF16),
        ),
        in_specs=[VMEM, VMEM, VMEM, VMEM, ANY, VMEM, VMEM],
        out_specs=(VMEM,) * 4,
        scratch_shapes=[
            pltpu.VMEM((16, PAD, LEN), BF16),
            pltpu.VMEM((16, PAD, INNER_DEV), BF16),
            pltpu.VMEM((16, PAD, INNER_DEV), BF16),
            pltpu.VMEM((2, 4, HEAD, INNER_DEV), BF16),
            pltpu.VMEM((2, 4, PAD, INNER_DEV), BF16),
            pltpu.VMEM((3, PAD, INNER_DEV), BF16),
            pltpu.VMEM((2, HEAD, INNER_DEV), BF16),
            pltpu.VMEM((2, PAD, INNER_DEV), BF16),
            pltpu.VMEM((2, PAD, LEN), BF16),
            pltpu.VMEM((16, LEN), BF16),
            pltpu.VMEM((LEN, INNER_DEV), F32),
            pltpu.VMEM((PAD, INNER_DEV), F32),
            dma((14,)), dma((16,)), dma((2, 4)), dma((2, 4)), dma((2, 4)), dma((2, 4)),
            dma((4,)), dma((4,)), dma((4,)), dma((1,)),
        ],
        compiler_params=pltpu.CompilerParams(
            collective_id=1, has_side_effects=True, vmem_limit_bytes=LIMIT
        ),
    )(*operands)


def per_device(byte_rows, context, weight, keep_list, counts, gate_vector):
    context_rows = context[0, 0]
    kept = jnp.where(lax.broadcasted_iota(jnp.int32, (1, LEN), 1) < counts[:, None], keep_list, -1)
    pad = ((0, 0), (0, PAD - SLAB), (0, 0))
    byte_slabs = jnp.pad(byte_rows[0, 0].T.reshape(2, SLAB, LEN), pad)
    gate_column = jnp.pad(gate_vector.reshape(2, SLAB, 1), pad)
    weight_rows = jnp.pad(weight[0], pad[1:])
    grad, e, proj, gate, weight_full = forward_call(
        weight_rows, context_rows, byte_slabs, gate_column, kept.reshape(LEN, 1), kept
    )
    rows, gate_out, context_grad, weight_grad = backward_call(
        grad, e, proj, gate, weight_full, context_rows, kept
    )
    section_rows = rows[:, :SLAB].reshape(2 * SLAB, LEN).T[None, None]
    return (
        section_rows,
        gate_out[0:1][None],
        context_grad[None, None],
        weight_grad[None, :SLAB],
    )


def solution(mesh):
    placed = (
        P("section", "dp", None, "tensor"),
        P("section", "dp", None, "tensor"),
        P("section", "dp", "tensor"),
        P("dp", None),
        P("dp"),
        P("tensor"),
    )
    return jax.shard_map(
        per_device,
        mesh=mesh,
        in_specs=placed,
        out_specs=(
            P("section", "dp", None, "tensor"),
            P("section", "dp", None),
            P("section", "dp", None, "tensor"),
            P("section", "dp", "tensor"),
        ),
        check_vma=False,
    )
```

time: 417 us -> 204 us (0.49)
  the two profiles are of different devices: /device:TPU:19 before, /device:TPU:56 now
where the time goes in v1:
time: 204 us; the launch traced here: 203 us
  Pallas kernels  187 us (92%)
  local copies, waits for them, and re-layouts  13.2 us (6%)
    pallas_call x1, Pallas kernels, backward_call(): pl.pallas_call(backward_kernel, name='backward', out_shape=(jax.ShapeDtyp...  120 us
    pallas_call x1, Pallas kernels, forward_call(): pl.pallas_call(forward_kernel, name='forward', out_shape=(jax.ShapeDtypeS...  67.3 us

profile of v1, /device:TPU:56, one launch (start us, length us, event | category | flops | bytes accessed | tf_op | source)
XLA Modules:
  0.0 203.3 jit_solution(18388904160385728552)
XLA Ops:
  1.3 1.3 compare_select_fusion.krow_ref
  2.5 0.7 fusion
  3.2 0.9 copy.11.kcol_ref
  4.1 0.9 reshape.35
  5.0 0.7 pad.14.g_ref
  5.7 1.7 pad.12.w_ref
  7.4 1.2 reshape.31
  8.6 0.9 pad.13.byte_ref
  9.5 67.3 %forward.1 = (bf16[2,304,512]{2,1,0:T(8,128)(2,1)}, bf16[2,304,512]{2,1,0:T(8,128)(2,1)}, f32[2,304,512]{2,1,0:T(8,128)}, bf16[16,512]{1,0:T(8,128)(2,1)}, bf16[16,304,512]{2,1,0:T(8,128)(2,1)}) custom-call(bf16[304,512]{1,0:T(8,128)(2,1)} %pad.12.w_ref, bf16[512,512]{1,0:T(8,128)(2,1)} %bitcast.18, bf16[2,304,512]{2,1,0:T(8,128)(2,1)} %pad.13.byte_ref, ...), custom_call_target="tpu_custom_call" | custom-call | tf_op jit(solution)/shard_map/forward/pallas_call | solution.py:511
  76.8 119.7 %backward.1 = (bf16[2,304,512]{2,1,0:T(8,128)(2,1)}, bf16[16,512]{1,0:T(8,128)(2,1)}, bf16[512,512]{1,0:T(8,128)(2,1)}, bf16[304,512]{1,0:T(8,128)(2,1)}) custom-call(bf16[2,304,512]{2,1,0:T(8,128)(2,1)} %get-tuple-element.13.grad_ref, bf16[2,304,512]{2,1,0:T(8,128)(2,1)} %get-tuple-element.14.e_ref, f32[2,304,512]{2,1,0:T(8,128)} %get-tuple-element.15.proj_ref, ...), custom_call_target="tpu_custom_call" | custom-call | tf_op jit(solution)/shard_map/backward/pallas_call | solution.py:543
  196.4 1.1 slice.9
  197.6 0.9 reshape.34
  198.5 1.3 slice_bitcast_fusion.1
  199.8 1.7 slice_bitcast_fusion
  201.5 1.9 copy.14

commit v2 on v0

v2 whole, which is shorter than its diff:
```python
import jax
import jax.numpy as jnp
from jax import lax
from jax.experimental import pallas as pl
from jax.experimental.pallas import tpu as pltpu
from jax.sharding import PartitionSpec as P

D = 4672
SLAB = 292
PAD = 304
COLS = 2 * SLAB
LEN = 512
INNER_DEV = 512
EPSILON = 1e-06
SHARPNESS = 30.0

MESH = pl.DeviceIdType.MESH
F32 = jnp.float32
BF16 = jnp.bfloat16


def turn(i, step):
    return lax.rem(i + step, 4)


def send(src, dst, send_sem, recv_sem, to):
    return pltpu.make_async_remote_copy(
        src_ref=src,
        dst_ref=dst,
        send_sem=send_sem,
        recv_sem=recv_sem,
        device_id=to,
        device_id_type=MESH,
    )


def contract(a, b, axis_a, axis_b):
    return lax.dot_general(
        a, b, (((axis_a,), (axis_b,)), ((), ())), preferred_element_type=F32
    )


def kernel(
    byte_ref, ctx_ref, w_ref, keep_ref, counts_ref, g_ref,
    rows_ref, gates_ref, cgrad_ref, wgrad_ref,
    stage, wf, cf, bt, gcol, pacc, spread, e_ref, gt, st_out, st_in, gate_out, gate_in, xin,
    wp, yh, yr, zh, zr, base, final, wg, q, qa, qb,
    ws, wr, ps, pr, cs_, cr, xs, ss, sr, hs, hr, fs, fr, zs, zrs, qs, qr, os_, or_, ready,
):
    s = lax.axis_index("section")
    d = lax.axis_index("dp")
    t = lax.axis_index("tensor")
    y, z, x, c = lax.div(d, 4), lax.rem(d, 4), lax.div(t, 2), lax.rem(t, 2)

    def device(yy, zz, xx, cc):
        return (s, yy * 4 + zz, xx * 2 + cc)

    up, down = device(turn(y, 1), z, x, c), device(turn(y, 3), z, x, c)
    right, left = device(y, turn(z, 1), x, c), device(y, turn(z, 3), x, c)
    east, west = device(y, z, turn(x, 1), c), device(y, z, turn(x, 3), c)
    sibling = device(y, z, x, 1 - c)
    partner = (1 - s, d, t)
    team = [(s, d, lax.rem(t + j, 8)) for j in range(1, 8)]
    holder = device(x, z, y, lax.div(z, 2))
    owns = lax.div(z, 2) == c
    diagonal = x == y
    stays = jnp.logical_and(diagonal, owns)

    barrier = pltpu.get_barrier_semaphore()
    hello = [up, down, right, left, partner] + team
    for peer in hello:
        pl.semaphore_signal(barrier, inc=1, device_id=peer, device_id_type=MESH)

    @pl.when(jnp.logical_not(stays))
    def _():
        pl.semaphore_signal(barrier, inc=1, device_id=holder, device_id_type=MESH)

    for core in range(2):
        @pl.when(jnp.logical_and(owns, jnp.logical_not(jnp.logical_and(diagonal, c == core))))
        def _():
            pl.semaphore_signal(
                barrier, inc=1, device_id=device(x, z, y, core), device_id_type=MESH
            )

    stage[pl.ds(PAD - 16, 16)] = jnp.zeros((16, INNER_DEV), BF16)
    stage[pl.ds(0, SLAB)] = w_ref[0]
    cf[t] = ctx_ref[0, 0]
    fold = []
    for i in range(2):
        row = lax.broadcasted_iota(jnp.int32, (PAD, COLS), 0)
        col = lax.broadcasted_iota(jnp.int32, (PAD, COLS), 1)
        hit = jnp.logical_and(col == row + i * SLAB, row < SLAB)
        fold.append(jnp.where(hit, 1.0, 0.0).astype(BF16))
    for i in range(2):
        bt[i] = contract(fold[i], byte_ref[0, 0], 1, 1).astype(BF16)

    greeted = (
        len(hello)
        + jnp.where(stays, 0, 1)
        + jnp.where(owns, jnp.where(diagonal, 1, 2), 0)
    )
    pl.semaphore_wait(barrier, greeted)

    def unit(yy, zz):
        return yy * 4 + zz * 2

    def pair(ref, n):
        return ref.at[pl.ds(n, 2)]

    always = []

    def go(copy):
        copy.start()
        always.append(copy)

    def start(copies):
        for copy in copies:
            copy.start()

    home = x * 4 + lax.rem(z, 2) * 2 + c
    to_holder = send(stage, wf.at[home], ps.at[2], wr.at[home], holder)

    @pl.when(stays)
    def _():
        wf[home] = stage[...]

    @pl.when(jnp.logical_not(stays))
    def _():
        to_holder.start()

    rows_in = send(bt, xin, xs.at[0], xs.at[1], partner)
    rows_back = send(e_ref, xin, xs.at[0], xs.at[1], partner)
    gates_back = send(gate_out, gate_in, xs.at[2], xs.at[3], partner)

    @pl.when(s == 1)
    def _():
        rows_in.start()

    odd = lax.rem(z, 2)
    zz1 = jnp.where(owns, odd, 1 - odd)
    zz2 = 1 - zz1
    near = 1 - odd
    from_left = owns == (odd == 1)
    half = LEN // 2

    def context_out():
        for i, to in enumerate((east, west, sibling)):
            go(send(ctx_ref.at[0, 0], cf.at[t], cs_.at[i], cr.at[t, 0], to))

    def wait_context(it, part):
        rows = cf.at[it]
        if part is not None:
            rows = cf.at[it, pl.ds(part * half, half)]
        send(rows, rows, cs_.at[0], cr.at[it, part or 0], east).wait_recv()

    def context_on():
        for i, (xx, to) in enumerate(((turn(x, 3), east), (turn(x, 1), west))):
            it = xx * 2 + c
            wait_context(it, None)
            rows = cf.at[it, pl.ds(i * half, half)]
            go(send(rows, rows, cs_.at[3 + i], cr.at[it, i], to))
            go(send(cf.at[it], cf.at[it], cs_.at[5 + i], cr.at[it, 0], sibling))

    def context_last():
        it = turn(x, 2) * 2 + c
        wait_context(it, 0)
        wait_context(it, 1)
        go(send(cf.at[it], cf.at[it], cs_.at[7], cr.at[it, 0], sibling))
        for xx in range(4):
            wait_context(xx * 2 + 1 - c, None)

    def arrived(n):
        send(pair(wf, n), pair(wf, n), ws.at[0], wr.at[n], up).wait_recv()

    def arrived_block(n):
        send(wf.at[n], wf.at[n], ws.at[0], wr.at[n], up).wait_recv()

    def along_y(zz, u):
        n = unit(y, zz)
        return (
            send(pair(wf, n), pair(wf, n), ws.at[4 + 4 * u], wr.at[n], up),
            send(pair(wf, n), pair(wf, n), ws.at[5 + 4 * u], wr.at[n], down),
        )

    def beyond_y(zz, u):
        n, m = unit(turn(y, 3), zz), unit(turn(y, 1), zz) + 1
        return (
            send(wf.at[n], wf.at[n], ws.at[6 + 4 * u], wr.at[n], up),
            send(wf.at[m], wf.at[m], ws.at[7 + 4 * u], wr.at[m], down),
        )

    def on_along_y(zz, u):
        ahead, back = beyond_y(zz, u)
        arrived(unit(turn(y, 3), zz))
        ahead.start()
        arrived(unit(turn(y, 1), zz))
        back.start()

    def along_z():
        n = unit(y, odd)
        return (
            send(pair(wf, n), pair(wf, n), ws.at[1], wr.at[n], right),
            send(pair(wf, n), pair(wf, n), ws.at[2], wr.at[n], left),
        )

    def arrived_far(yy, zz):
        n = unit(yy, zz)
        arrived_block(n)
        arrived_block(n + 1)

    onward = (
        send(wf.at[unit(y, near)], wf.at[unit(y, near)], ws.at[3], wr.at[unit(y, near)], right),
        send(
            wf.at[unit(y, near) + 1], wf.at[unit(y, near) + 1],
            ws.at[3], wr.at[unit(y, near) + 1], left,
        ),
    )

    def on_along_z():
        arrived(unit(y, near))

        @pl.when(from_left)
        def _():
            onward[0].start()

        @pl.when(jnp.logical_not(from_left))
        def _():
            onward[1].start()

    def project(yy, zz):
        n = unit(yy, zz)
        pacc[zz] += contract(wf[n], cf[yy * 2], 1, 1) + contract(wf[n + 1], cf[yy * 2 + 1], 1, 1)

    pacc[...] = jnp.zeros_like(pacc)

    @pl.when(owns)
    def _():
        for core in range(2):
            @pl.when(jnp.logical_not(jnp.logical_and(diagonal, c == core)))
            def _():
                arrived_block(unit(y, zz1) + core)
        start(along_z())
        start(along_y(zz1, 0))
        pl.semaphore_signal(ready, inc=1, device_id=sibling, device_id_type=MESH)

    @pl.when(jnp.logical_not(owns))
    def _():
        pl.semaphore_wait(ready, 1)

    context_out()

    @pl.when(owns)
    def _():
        on_along_y(zz1, 0)
        on_along_z()
        start(along_y(zz2, 1))

    @pl.when(jnp.logical_not(owns))
    def _():
        on_along_z()
        start(along_y(zz1, 0))

    context_on()

    @pl.when(jnp.logical_not(owns))
    def _():
        arrived_far(y, zz2)
        start(along_y(zz2, 1))

    context_last()

    pick = jnp.where(
        lax.broadcasted_iota(jnp.int32, (1, LEN), 1) < counts_ref[0], keep_ref[...], -1
    )
    live = pick >= 0
    place_of = lax.broadcasted_iota(jnp.int32, (LEN, LEN), 0)
    picks = jnp.where(pick == place_of, 1.0, 0.0).astype(BF16)

    project(y, zz1)
    project(y, zz2)

    @pl.when(owns)
    def _():
        arrived_far(turn(y, 2), zz1)

    @pl.when(jnp.logical_not(owns))
    def _():
        on_along_y(zz1, 0)

    project(turn(y, 1), zz1)
    project(turn(y, 3), zz1)

    @pl.when(owns)
    def _():
        on_along_y(zz2, 1)

    @pl.when(jnp.logical_not(owns))
    def _():
        on_along_y(zz2, 1)
        arrived_far(turn(y, 2), zz1)

    @pl.when(s == 0)
    def _():
        rows_in.wait_recv()
        for i in range(2):
            spread[i] = contract(xin[i], picks, 1, 1).astype(BF16)

    g = g_ref[...]
    first = g.astype(BF16)
    rest = g - first.astype(F32)
    second = rest.astype(BF16)
    third = (rest - second.astype(F32)).astype(BF16)
    for i in range(2):
        terms = [contract(fold[i], jnp.broadcast_to(v, (16, COLS)), 1, 1) for v in (first, second, third)]
        gcol[i] = (terms[0] + terms[1] + terms[2])[:, 0:1]

    project(turn(y, 1), zz2)
    project(turn(y, 3), zz2)
    project(turn(y, 2), zz1)
    arrived_far(turn(y, 2), zz2)
    project(turn(y, 2), zz2)

    @pl.when(s == 0)
    def _():
        st_out[...] = jnp.zeros_like(st_out)
        for i in range(2):
            e = (bt[i].astype(F32) + pacc[i]).astype(BF16)
            e_ref[i] = e
            e = e.astype(F32)
            st_out[0:1] += jnp.sum(e * e, axis=0, keepdims=True)
            st_out[1:2] += jnp.sum(e * gcol[i], axis=0, keepdims=True)
        st_in[t] = st_out[...]
        stats = [
            send(st_out, st_in.at[t], ss.at[j], sr.at[j], peer) for j, peer in enumerate(team)
        ]
        for copy in stats:
            copy.start()
        rows_back.start()
        for copy in stats:
            copy.wait()
        sums = st_in[0]
        for j in range(1, 8):
            sums = sums + st_in[j]
        inverse = lax.rsqrt(sums[0:1] / D + EPSILON)
        score = inverse * sums[1:2]
        squashed = jax.nn.sigmoid(score)
        gate = (-SHARPNESS * squashed).astype(BF16)
        gate_out[...] = jnp.broadcast_to(gate, gate_out.shape)
        gates_back.start()
        slope = -SHARPNESS * squashed * (1.0 - squashed)
        pull = score * inverse * inverse / D
        for i in range(2):
            gate_part = slope * (inverse * gcol[i] - pull * e_ref[i].astype(F32))
            gt[i] = (spread[i].astype(F32) + gate_part).astype(BF16)

    @pl.when(s == 1)
    def _():
        for i in range(2):
            rows = bt[i]
            gt[i] = jnp.where(live, rows, jnp.zeros_like(rows))

    zza = jnp.where(owns, near, odd)
    zzb = 1 - zza

    def products(yy, zz):
        n = unit(yy, zz)
        for core in range(2):
            wp[n + core] = jnp.dot(
                gt[zz], cf[yy * 2 + core], preferred_element_type=F32
            ).astype(BF16)

    def halves(zz):
        n = unit(turn(y, 2), zz)
        return (
            send(wp.at[n], yh.at[0, zz], hs.at[0, zz], hr.at[0, zz], up),
            send(wp.at[n + 1], yh.at[1, zz], hs.at[1, zz], hr.at[1, zz], down),
        )

    def ways(zz):
        return (
            send(pair(wp, unit(turn(y, 1), zz)), yr.at[0, zz], fs.at[0, zz], fr.at[0, zz], up),
            send(pair(wp, unit(turn(y, 3), zz)), yr.at[1, zz], fs.at[1, zz], fr.at[1, zz], down),
        )

    def merge(zz):
        to_up, to_down = halves(zz)
        on_up, on_down = ways(zz)
        n = unit(turn(y, 1), zz)
        to_up.wait_recv()
        wp[n] = (wp[n].astype(F32) + yh[0, zz].astype(F32)).astype(BF16)
        on_up.start()
        n = unit(turn(y, 3), zz) + 1
        to_down.wait_recv()
        wp[n] = (wp[n].astype(F32) + yh[1, zz].astype(F32)).astype(BF16)
        on_down.start()

    products(turn(y, 2), zza)
    start(halves(zza))
    products(turn(y, 2), zzb)
    start(halves(zzb))
    products(turn(y, 1), zza)
    products(turn(y, 3), zza)
    merge(zza)
    products(turn(y, 1), zzb)
    products(turn(y, 3), zzb)
    merge(zzb)
    products(y, zza)
    products(y, zzb)

    def to_sibling(xx):
        return send(q.at[xx * 2 + 1 - c], qa.at[xx], qs.at[xx], qr.at[xx], sibling)

    def to_column(xx):
        return send(q.at[xx * 2 + c], qb.at[x], os_.at[xx], or_.at[x], device(y, z, xx, c))

    def context_part(it):
        n = lax.div(it, 2) * 4 + lax.rem(it, 2)
        return contract(gt[0], wf[n], 0, 0) + contract(gt[1], wf[n + 2], 0, 0)

    @pl.loop(0, 4)
    def _(j):
        xx = turn(x, j + 1)
        q[xx * 2 + 1 - c] = context_part(xx * 2 + 1 - c).astype(BF16)
        to_sibling(xx).start()

    @pl.loop(0, 4)
    def _(j):
        xx = turn(x, j + 1)
        part = context_part(xx * 2 + c)
        to_sibling(xx).wait_recv()
        q[xx * 2 + c] = (part + qa[xx].astype(F32)).astype(BF16)

        @pl.when(j < 3)
        def _():
            to_column(xx).start()

    def summed(zz, core):
        n = unit(y, zz) + core
        return wp[n].astype(F32) + yr[0, zz, core].astype(F32) + yr[1, zz, core].astype(F32)

    def wait_ways(zz):
        for copy in ways(zz):
            copy.wait_recv()

    far_z = (
        send(base.at[odd, 0], zh.at[0], zs.at[0], zrs.at[0], right),
        send(base.at[odd, 1], zh.at[1], zs.at[1], zrs.at[1], left),
    )
    near_z = (
        send(base.at[near], zr.at[0], zs.at[2], zrs.at[2], right),
        send(base.at[near], zr.at[1], zs.at[3], zrs.at[3], left),
    )

    def total_y(zz):
        wait_ways(zz)
        for core in range(2):
            base[zz, core] = summed(zz, core).astype(BF16)

    def near_on():
        @pl.when(from_left)
        def _():
            far_z[1].wait_recv()
            base[near, 1] = (base[near, 1].astype(F32) + zh[1].astype(F32)).astype(BF16)
            near_z[1].start()

        @pl.when(jnp.logical_not(from_left))
        def _():
            far_z[0].wait_recv()
            base[near, 0] = (base[near, 0].astype(F32) + zh[0].astype(F32)).astype(BF16)
            near_z[0].start()

    total_y(zza)

    @pl.when(jnp.logical_not(owns))
    def _():
        start(far_z)

    rows_t = xin

    @pl.when(s == 0)
    def _():
        rows_t[...] = gt[...]
        gates_ref[0] = gate_out[0:1]

    @pl.when(s == 1)
    def _():
        rows_back.wait_recv()
        gates_back.wait_recv()
        for i in range(2):
            packed = jnp.dot(xin[i], picks, preferred_element_type=F32)
            rows_t[i] = jnp.where(live, packed + pacc[i], 0.0).astype(BF16)
        gates_ref[0] = jnp.dot(gate_in[...], picks, preferred_element_type=F32).astype(BF16)[0:1]

    rows_ref[0, 0] = (
        contract(rows_t[0], fold[0], 0, 0) + contract(rows_t[1], fold[1], 0, 0)
    ).astype(BF16)

    total_y(zzb)
    near_on()

    total = q[x * 2 + c].astype(F32)
    for step in range(1, 4):
        xx = turn(x, step)
        send(qb.at[xx], qb.at[xx], os_.at[0], or_.at[xx], east).wait_recv()
        total = total + qb[xx].astype(F32)
    cgrad_ref[0, 0] = total.astype(BF16)

    def homeward(core):
        return send(final.at[core], wg, ps.at[core], pr.at[0], device(x, z, y, core))

    @pl.when(owns)
    def _():
        near_z[0].wait_recv()
        near_z[1].wait_recv()
        for core in range(2):
            final[core] = (
                base[odd, core].astype(F32) + zr[0, core].astype(F32) + zr[1, core].astype(F32)
            ).astype(BF16)
            here = jnp.logical_and(diagonal, c == core)

            @pl.when(here)
            def _():
                wg[...] = final[core]

            @pl.when(jnp.logical_not(here))
            def _():
                homeward(core).start()

    @pl.when(jnp.logical_not(stays))
    def _():
        send(stage, wg, ps.at[0], pr.at[0], holder).wait_recv()

    wgrad_ref[0] = wg[pl.ds(0, SLAB)]

    @pl.when(owns)
    def _():
        for core in range(2):
            @pl.when(jnp.logical_not(jnp.logical_and(diagonal, c == core)))
            def _():
                homeward(core).wait_send()
        for copy in along_z():
            copy.wait_send()

    @pl.when(jnp.logical_not(owns))
    def _():
        for copy in far_z:
            copy.wait_send()

    @pl.when(from_left)
    def _():
        onward[0].wait_send()
        near_z[1].wait_send()

    @pl.when(jnp.logical_not(from_left))
    def _():
        onward[1].wait_send()
        near_z[0].wait_send()

    for copy in always:
        copy.wait_send()
    for zz, u in ((zz1, 0), (zz2, 1)):
        for copy in along_y(zz, u) + beyond_y(zz, u) + halves(zz) + ways(zz):
            copy.wait_send()

    @pl.when(jnp.logical_not(stays))
    def _():
        to_holder.wait_send()

    for step in range(4):
        to_sibling(turn(x, step)).wait_send()
        if step:
            to_column(turn(x, step)).wait_send()

    @pl.when(s == 0)
    def _():
        rows_back.wait_send()
        gates_back.wait_send()

    @pl.when(s == 1)
    def _():
        rows_in.wait_send()


def call(*operands):
    dma = pltpu.SemaphoreType.DMA
    vmem = pl.BlockSpec(memory_space=pltpu.VMEM)

    def block(*lead, kind=BF16):
        return pltpu.VMEM((*lead, PAD, LEN), kind)

    return pl.pallas_call(
        kernel,
        name="relay",
        out_shape=(
            jax.ShapeDtypeStruct((1, 1, LEN, COLS), BF16),
            jax.ShapeDtypeStruct((1, 1, LEN), BF16),
            jax.ShapeDtypeStruct((1, 1, LEN, INNER_DEV), BF16),
            jax.ShapeDtypeStruct((1, SLAB, INNER_DEV), BF16),
        ),
        in_specs=[vmem] * 4 + [pl.BlockSpec(memory_space=pltpu.SMEM), vmem],
        out_specs=(vmem,) * 4,
        scratch_shapes=[
            block(),
            block(16),
            pltpu.VMEM((8, LEN, INNER_DEV), BF16),
            block(2),
            pltpu.VMEM((2, PAD, 1), F32),
            block(2, kind=F32),
            block(2),
            block(2),
            block(2),
            pltpu.VMEM((8, LEN), F32),
            pltpu.VMEM((8, 8, LEN), F32),
            pltpu.VMEM((16, LEN), BF16),
            pltpu.VMEM((16, LEN), BF16),
            block(2),
            block(16),
            block(2, 2),
            block(2, 2, 2),
            block(2),
            block(2, 2),
            block(2, 2),
            block(2),
            block(),
            pltpu.VMEM((8, LEN, INNER_DEV), BF16),
            pltpu.VMEM((4, LEN, INNER_DEV), BF16),
            pltpu.VMEM((4, LEN, INNER_DEV), BF16),
            dma((12,)), dma((16,)), dma((3,)), dma((1,)), dma((8,)), dma((8, 2)), dma((4,)),
            dma((7,)), dma((7,)), dma((2, 2)), dma((2, 2)), dma((2, 2)), dma((2, 2)),
            dma((4,)), dma((4,)), dma((4,)), dma((4,)), dma((4,)), dma((4,)),
            pltpu.SemaphoreType.REGULAR,
        ],
        compiler_params=pltpu.CompilerParams(
            collective_id=0, has_side_effects=True, vmem_limit_bytes=56 * 2**20
        ),
    )(*operands)


def per_device(byte_rows, context, weight, keep_list, counts, gate_vector):
    return call(byte_rows, context, weight, keep_list, counts, gate_vector.reshape(1, COLS))


def solution(mesh):
    placed = (
        P("section", "dp", None, "tensor"),
        P("section", "dp", None, "tensor"),
        P("section", "dp", "tensor"),
        P("dp", None),
        P("dp"),
        P("tensor"),
    )
    return jax.shard_map(
        per_device,
        mesh=mesh,
        in_specs=placed,
        out_specs=(
            P("section", "dp", None, "tensor"),
            P("section", "dp", None),
            P("section", "dp", None, "tensor"),
            P("section", "dp", "tensor"),
        ),
        check_vma=False,
    )
```

time: 417 us -> 161 us (0.39)
  waiting for transfers between devices: 201 us -> 0 us
  Pallas kernels: 0 us -> 149 us
  blocking collectives: 136 us -> 0 us
  matrix products: 23.6 us -> 0 us
  between operations: 15.3 us -> 1.31 us
  other arithmetic: 13.2 us -> 0 us
  local copies, waits for them, and re-layouts: 17.3 us -> 8.06 us
  starting transfers between devices: 6.73 us -> 0 us
    all_gather x2 -> x0, waiting for transfers between devices: 156 us -> none  [the longest x1 124 us: per_device(): full_weight = lax.all_gather(weight[0], 'dp', axis=0, tiled=True)]
    pallas_call x0 -> x1, Pallas kernels: none -> 149 us  [call(): pl.pallas_call(kernel, name='relay', out_shape=(jax.ShapeDtypeStruct((1,...]
    unnamed x1 -> x0, blocking collectives: 123 us -> none
    reduce_scatter x1 -> x0, waiting for transfers between devices: 44.6 us -> none  [per_device(): lax.psum_scatter(projected_part.astype(jnp.bfloat16), 'tensor', scatter_d...]
    dot_general x3 -> x0, matrix products: 23.6 us -> none  [the longest x1 8.73 us: per_device(): jnp.einsum('bpd,di->bpi', gathered, full_weight, preferred_element_type=j...]
    psum x1 -> x0, blocking collectives: 13.1 us -> none  [per_device(): lax.psum((jnp.sum(hidden_wide * hidden_wide, axis=-1), jnp.sum(hidden_wid...]
    gather x3 -> x0, local copies, waits for them, and re-layouts: 7.26 us -> none  [pick_rows(): return table[index]]
    scatter-add x2 -> x0, other arithmetic: 5.19 us -> none  [spread_rows(): return jnp.zeros(values.shape, jnp.float32).at[index].add(values)]
  transfers between devices with their start and end apart: 6 -> 0, of which waited for: 4 -> 0; matrix products, arithmetic and copies ran while one was open for 4% -> 0% of each run, Pallas kernels for 0% -> 0%
where the time goes in v2:
time: 161 us; the launch traced here: 158 us
  Pallas kernels  149 us (93%)
  local copies, waits for them, and re-layouts  8.06 us (5%)
    pallas_call x1, Pallas kernels, call(): pl.pallas_call(kernel, name='relay', out_shape=(jax.ShapeDtypeStruct((1,...  149 us
    unnamed x10, local copies, waits for them, and re-layouts  4.6 us

profile of v2, /device:TPU:19, one launch (start us, length us, event | category | flops | bytes accessed | tf_op | source)
XLA Modules:
  0.0 158.5 jit_solution(2121446718299446083)
XLA Ops:
  1.3 1.3 reshape.11.g_ref
  2.5 2.1 %copy.10.byte_ref = bf16[1,1,512,584]{3,2,1,0:T(8,128)(2,1)} copy(bf16[1,1,512,584]{2,3,1,0:T(8,128)(2,1)} %param.6) | data formatting | bytes 1196032 | tf_op args[0]
  4.7 149.1 %relay.1 = (bf16[1,1,512,584]{3,2,1,0:T(8,128)(2,1)}, bf16[1,1,512]{2,1,0:T(2,128)(2,1)}, bf16[1,1,512,512]{3,2,1,0:T(8,128)(2,1)}, bf16[1,292,512]{2,1,0:T(8,128)(2,1)}) custom-call(bf16[1,1,512,584]{3,2,1,0:T(8,128)(2,1)} %copy.10.byte_ref, bf16[1,1,512,512]{3,2,1,0:T(8,128)(2,1)} %ctx_ref.1, bf16[1,292,512]{2,1,0:T(8,128)(2,1)} %w_ref.1, ...), custom_call_target="tpu_custom_call" | custom-call | tf_op jit(solution)/shard_map/relay/pallas_call | solution.py:591
  153.8 0.0 copy-start.2
  153.8 0.0 copy-start
  153.8 2.2 %copy.11 = bf16[1,1,512,584]{2,3,1,0:T(8,128)(2,1)} copy(bf16[1,1,512,584]{3,2,1,0:T(8,128)(2,1)} %get-tuple-element.4) | data formatting | bytes 1196032 | tf_op jit(solution)/shard_map/relay/pallas_call | solution.py:591
  156.0 0.0 copy-done.2
  156.0 0.6 copy.16
  156.6 0.0 copy-done
  156.6 0.0 copy-start.1
  156.6 0.8 copy.17
  157.4 0.4 copy-done.1
  157.8 0.7 copy.18
Async XLA Ops:
  153.8 2.2 %copy-start.2 = (bf16[1,1,512]{2,1,0:T(2,128)(2,1)S(1)}, bf16[1,1,512]{2,1,0:T(2,128)(2,1)}, u32[]{:S(2)}) copy-start(bf16[1,1,512]{2,1,0:T(2,128)(2,1)} %get-tuple-element.13) | copy-start | bytes 3076
  153.8 2.8 %copy-start = (bf16[1,1,512,512]{3,2,1,0:T(8,128)(2,1)S(1)}, bf16[1,1,512,512]{3,2,1,0:T(8,128)(2,1)}, u32[]{:S(2)}) copy-start(bf16[1,1,512,512]{3,2,1,0:T(8,128)(2,1)} %get-tuple-element.14) | copy-start | bytes 1572868
  156.6 1.2 copy-start.1

commit v3 on v2

--- a/solution.py
+++ b/solution.py
@@ -8,6 +8,7 @@
 D = 4672
 SLAB = 292
 PAD = 304
+START, SIZE = (0, 128, 240), (128, 112, 64)
 COLS = 2 * SLAB
 LEN = 512
 INNER_DEV = 512
@@ -44,8 +45,8 @@
     byte_ref, ctx_ref, w_ref, keep_ref, counts_ref, g_ref,
     rows_ref, gates_ref, cgrad_ref, wgrad_ref,
     stage, wf, cf, bt, gcol, pacc, spread, e_ref, gt, st_out, st_in, gate_out, gate_in, xin,
-    wp, yh, yr, zh, zr, base, final, wg, q, qa, qb,
-    ws, wr, ps, pr, cs_, cr, xs, ss, sr, hs, hr, fs, fr, zs, zrs, qs, qr, os_, or_, ready,
+    wp, yh, yr, zh, zr, zhb, zrb, base, final, wg, q, qa, qb,
+    ws, wr, ps, pr, cs_, cr, xs, ss, sr, hs, hr, fs, fr, zs, zrs, qs, qr, os_, or_, bs, vs, vr, ready,
 ):
     s = lax.axis_index("section")
     d = lax.axis_index("dp")
@@ -92,7 +93,7 @@
         hit = jnp.logical_and(col == row + i * SLAB, row < SLAB)
         fold.append(jnp.where(hit, 1.0, 0.0).astype(BF16))
     for i in range(2):
-        bt[i] = contract(fold[i], byte_ref[0, 0], 1, 1).astype(BF16)
+        bt[i] = jnp.dot(fold[i], byte_ref[...], preferred_element_type=F32).astype(BF16)
 
     greeted = (
         len(hello)
@@ -104,8 +105,11 @@
     def unit(yy, zz):
         return yy * 4 + zz * 2
 
-    def pair(ref, n):
-        return ref.at[pl.ds(n, 2)]
+    def pair(ref, n, h):
+        return ref.at[pl.ds(n, 2), pl.ds(START[h], SIZE[h])]
+
+    def one(ref, n, h):
+        return ref.at[n, pl.ds(START[h], SIZE[h])]
 
     always = []
 
@@ -118,7 +122,10 @@
             copy.start()
 
     home = x * 4 + lax.rem(z, 2) * 2 + c
-    to_holder = send(stage, wf.at[home], ps.at[2], wr.at[home], holder)
+
+    def to_holder(h):
+        rows = stage.at[pl.ds(START[h], SIZE[h])]
+        return send(rows, one(wf, home, h), ps.at[2, h], wr.at[home, h], holder)
 
     @pl.when(stays)
     def _():
@@ -126,7 +133,7 @@
 
     @pl.when(jnp.logical_not(stays))
     def _():
-        to_holder.start()
+        to_holder(0).start()
 
     rows_in = send(bt, xin, xs.at[0], xs.at[1], partner)
     rows_back = send(e_ref, xin, xs.at[0], xs.at[1], partner)
@@ -169,63 +176,82 @@
         for xx in range(4):
             wait_context(xx * 2 + 1 - c, None)
 
-    def arrived(n):
-        send(pair(wf, n), pair(wf, n), ws.at[0], wr.at[n], up).wait_recv()
-
-    def arrived_block(n):
-        send(wf.at[n], wf.at[n], ws.at[0], wr.at[n], up).wait_recv()
-
-    def along_y(zz, u):
+    def arrived(n, h):
+        send(pair(wf, n, h), pair(wf, n, h), ws.at[0, h], wr.at[n, h], up).wait_recv()
+
+    def arrived_block(n, h):
+        send(one(wf, n, h), one(wf, n, h), ws.at[0, h], wr.at[n, h], up).wait_recv()
+
+    def pass_pair(n, h, i, to):
+        return send(pair(wf, n, h), pair(wf, n, h), ws.at[i, h], wr.at[n, h], to)
+
+    def pass_one(n, h, i, to):
+        return send(one(wf, n, h), one(wf, n, h), ws.at[i, h], wr.at[n, h], to)
+
+    def along_y(zz, u, h):
         n = unit(y, zz)
+        return pass_pair(n, h, 4 + 4 * u, up), pass_pair(n, h, 5 + 4 * u, down)
+
+    def beyond_y(zz, u, h):
+        n, m = unit(turn(y, 3), zz), unit(turn(y, 1), zz) + 1
+        return pass_one(n, h, 6 + 4 * u, up), pass_one(m, h, 7 + 4 * u, down)
+
+    def on_along_y(zz, u, h):
+        ahead, back = beyond_y(zz, u, h)
+        arrived(unit(turn(y, 3), zz), h)
+        ahead.start()
+        arrived(unit(turn(y, 1), zz), h)
+        back.start()
+
+    def along_z(h):
+        n = unit(y, odd)
+        return pass_pair(n, h, 1, right), pass_pair(n, h, 2, left)
+
+    def arrived_far(yy, zz, h):
+        n = unit(yy, zz)
+        arrived_block(n, h)
+        arrived_block(n + 1, h)
+
+    def onward(h):
+        n = unit(y, near)
+        return pass_one(n, h, 3, right), pass_one(n + 1, h, 3, left)
+
+    def on_along_z(h):
+        arrived(unit(y, near), h)
+
+        @pl.when(from_left)
+        def _():
+            onward(h)[0].start()
+
+        @pl.when(jnp.logical_not(from_left))
+        def _():
+            onward(h)[1].start()
+
+    def last_z(step):
+        n = unit(turn(y, step), odd)
         return (
-            send(pair(wf, n), pair(wf, n), ws.at[4 + 4 * u], wr.at[n], up),
-            send(pair(wf, n), pair(wf, n), ws.at[5 + 4 * u], wr.at[n], down),
+            send(pair(wf, n, 2), pair(wf, n, 2), bs.at[0, step], wr.at[n, 2], right),
+            send(pair(wf, n, 2), pair(wf, n, 2), bs.at[1, step], wr.at[n, 2], left),
         )
 
-    def beyond_y(zz, u):
-        n, m = unit(turn(y, 3), zz), unit(turn(y, 1), zz) + 1
+    def last_onward(step):
+        n = unit(turn(y, step), near)
+        m = n + 1
         return (
-            send(wf.at[n], wf.at[n], ws.at[6 + 4 * u], wr.at[n], up),
-            send(wf.at[m], wf.at[m], ws.at[7 + 4 * u], wr.at[m], down),
+            send(one(wf, n, 2), one(wf, n, 2), bs.at[2, step], wr.at[n, 2], right),
+            send(one(wf, m, 2), one(wf, m, 2), bs.at[2, step], wr.at[m, 2], left),
         )
 
-    def on_along_y(zz, u):
-        ahead, back = beyond_y(zz, u)
-        arrived(unit(turn(y, 3), zz))
-        ahead.start()
-        arrived(unit(turn(y, 1), zz))
-        back.start()
-
-    def along_z():
-        n = unit(y, odd)
-        return (
-            send(pair(wf, n), pair(wf, n), ws.at[1], wr.at[n], right),
-            send(pair(wf, n), pair(wf, n), ws.at[2], wr.at[n], left),
-        )
-
-    def arrived_far(yy, zz):
-        n = unit(yy, zz)
-        arrived_block(n)
-        arrived_block(n + 1)
-
-    onward = (
-        send(wf.at[unit(y, near)], wf.at[unit(y, near)], ws.at[3], wr.at[unit(y, near)], right),
-        send(
-            wf.at[unit(y, near) + 1], wf.at[unit(y, near) + 1],
-            ws.at[3], wr.at[unit(y, near) + 1], left,
-        ),
-    )
-
-    def on_along_z():
-        arrived(unit(y, near))
+    def last_on_along_z(step):
+        arrived(unit(turn(y, step), near), 2)
 
         @pl.when(from_left)
         def _():
-            onward[0].start()
+            last_onward(step)[0].start()
 
         @pl.when(jnp.logical_not(from_left))
         def _():
-            onward[1].start()
+            last_onward(step)[1].start()
 
     def project(yy, zz):
         n = unit(yy, zz)
@@ -233,41 +259,84 @@
 
     pacc[...] = jnp.zeros_like(pacc)
 
+    @pl.when(jnp.logical_not(stays))
+    def _():
+        for h in range(2):
+            to_holder(h).wait_send()
+            to_holder(h + 1).start()
+
     @pl.when(owns)
     def _():
-        for core in range(2):
-            @pl.when(jnp.logical_not(jnp.logical_and(diagonal, c == core)))
-            def _():
-                arrived_block(unit(y, zz1) + core)
-        start(along_z())
-        start(along_y(zz1, 0))
+        for h in range(3):
+            for core in range(2):
+                @pl.when(jnp.logical_not(jnp.logical_and(diagonal, c == core)))
+                def _():
+                    arrived_block(unit(y, zz1) + core, h)
+            if h < 2:
+                start(along_z(h))
+            start(along_y(zz1, 0, h))
         pl.semaphore_signal(ready, inc=1, device_id=sibling, device_id_type=MESH)
 
     @pl.when(jnp.logical_not(owns))
     def _():
+        on_along_z(0)
+        start(along_y(zz1, 0, 0))
         pl.semaphore_wait(ready, 1)
 
     context_out()
 
     @pl.when(owns)
     def _():
-        on_along_y(zz1, 0)
-        on_along_z()
-        start(along_y(zz2, 1))
+        for h in range(2):
+            on_along_y(zz1, 0, h)
+            on_along_z(h)
+            start(along_y(zz2, 1, h))
+        start(last_z(0))
+        on_along_y(zz1, 0, 2)
+        start(last_z(1))
+        start(last_z(3))
+        arrived_far(turn(y, 2), zz1, 2)
+        start(last_z(2))
 
     @pl.when(jnp.logical_not(owns))
     def _():
-        on_along_z()
-        start(along_y(zz1, 0))
-
+        arrived_far(y, zz2, 0)
+        start(along_y(zz2, 1, 0))
+        on_along_z(1)
+        start(along_y(zz1, 0, 1))
+        arrived_far(y, zz2, 1)
+        start(along_y(zz2, 1, 1))
+
+    last_on_along_z(0)
     context_on()
 
+    @pl.when(owns)
+    def _():
+        on_along_y(zz2, 1, 0)
+
     @pl.when(jnp.logical_not(owns))
     def _():
-        arrived_far(y, zz2)
-        start(along_y(zz2, 1))
-
+        on_along_y(zz1, 0, 0)
+
+    last_on_along_z(1)
+    last_on_along_z(3)
+
+    @pl.when(owns)
+    def _():
+        on_along_y(zz2, 1, 1)
+
+    @pl.when(jnp.logical_not(owns))
+    def _():
+        on_along_y(zz2, 1, 0)
+        on_along_y(zz1, 0, 1)
+
+    last_on_along_z(2)
     context_last()
+
+    @pl.when(jnp.logical_not(owns))
+    def _():
+        for step in (0, 1, 3):
+            arrived_far(turn(y, step), odd, 2)
 
     pick = jnp.where(
         lax.broadcasted_iota(jnp.int32, (1, LEN), 1) < counts_ref[0], keep_ref[...], -1
@@ -279,25 +348,22 @@
     project(y, zz1)
     project(y, zz2)
 
-    @pl.when(owns)
-    def _():
-        arrived_far(turn(y, 2), zz1)
-
     @pl.when(jnp.logical_not(owns))
     def _():
-        on_along_y(zz1, 0)
+        on_along_y(zz2, 1, 1)
 
     project(turn(y, 1), zz1)
     project(turn(y, 3), zz1)
-
-    @pl.when(owns)
-    def _():
-        on_along_y(zz2, 1)
+    for h in range(2):
+        arrived_far(turn(y, 2), zz1, h)
+    project(turn(y, 1), zz2)
+    project(turn(y, 3), zz2)
 
     @pl.when(jnp.logical_not(owns))
     def _():
-        on_along_y(zz2, 1)
-        arrived_far(turn(y, 2), zz1)
+        arrived_far(turn(y, 2), odd, 2)
+
+    project(turn(y, 2), zz1)
 
     @pl.when(s == 0)
     def _():
@@ -314,10 +380,8 @@
         terms = [contract(fold[i], jnp.broadcast_to(v, (16, COLS)), 1, 1) for v in (first, second, third)]
         gcol[i] = (terms[0] + terms[1] + terms[2])[:, 0:1]
 
-    project(turn(y, 1), zz2)
-    project(turn(y, 3), zz2)
-    project(turn(y, 2), zz1)
-    arrived_far(turn(y, 2), zz2)
+    arrived_far(turn(y, 2), zz2, 0)
+    arrived_far(turn(y, 2), zz2, 1)
     project(turn(y, 2), zz2)
 
     @pl.when(s == 0)
@@ -369,43 +433,114 @@
                 gt[zz], cf[yy * 2 + core], preferred_element_type=F32
             ).astype(BF16)
 
-    def halves(zz):
+    def halves(zz, h):
         n = unit(turn(y, 2), zz)
         return (
-            send(wp.at[n], yh.at[0, zz], hs.at[0, zz], hr.at[0, zz], up),
-            send(wp.at[n + 1], yh.at[1, zz], hs.at[1, zz], hr.at[1, zz], down),
+            send(one(wp, n, h), yh.at[0, zz, pl.ds(START[h], SIZE[h])], hs.at[0, zz, h], hr.at[0, zz, h], up),
+            send(one(wp, n + 1, h), yh.at[1, zz, pl.ds(START[h], SIZE[h])], hs.at[1, zz, h], hr.at[1, zz, h], down),
         )
 
-    def ways(zz):
+    def ways(zz, h):
+        n, m = unit(turn(y, 1), zz), unit(turn(y, 3), zz)
         return (
-            send(pair(wp, unit(turn(y, 1), zz)), yr.at[0, zz], fs.at[0, zz], fr.at[0, zz], up),
-            send(pair(wp, unit(turn(y, 3), zz)), yr.at[1, zz], fs.at[1, zz], fr.at[1, zz], down),
+            send(pair(wp, n, h), pair(yr, zz * 2, h), fs.at[0, zz, h], fr.at[0, zz, h], up),
+            send(pair(wp, m, h), pair(yr, 4 + zz * 2, h), fs.at[1, zz, h], fr.at[1, zz, h], down),
         )
 
-    def merge(zz):
-        to_up, to_down = halves(zz)
-        on_up, on_down = ways(zz)
+    def merge(zz, h):
+        rows = pl.ds(START[h], SIZE[h])
+        to_up, to_down = halves(zz, h)
+        on_up, on_down = ways(zz, h)
         n = unit(turn(y, 1), zz)
         to_up.wait_recv()
-        wp[n] = (wp[n].astype(F32) + yh[0, zz].astype(F32)).astype(BF16)
+        wp[n, rows] = (wp[n, rows].astype(F32) + yh[0, zz, rows].astype(F32)).astype(BF16)
         on_up.start()
         n = unit(turn(y, 3), zz) + 1
         to_down.wait_recv()
-        wp[n] = (wp[n].astype(F32) + yh[1, zz].astype(F32)).astype(BF16)
+        wp[n, rows] = (wp[n, rows].astype(F32) + yh[1, zz, rows].astype(F32)).astype(BF16)
         on_down.start()
 
+    rows2 = pl.ds(START[2], SIZE[2])
+
+    def last_far(step):
+        n = unit(turn(y, step), odd)
+        return (
+            send(one(wp, n, 2), zhb.at[step * 2], vs.at[0, step], vr.at[0, step], right),
+            send(one(wp, n + 1, 2), zhb.at[step * 2 + 1], vs.at[1, step], vr.at[1, step], left),
+        )
+
+    def last_near(step):
+        n = unit(turn(y, step), near)
+        return (
+            send(
+                pair(wp, n, 2), zrb.at[pl.ds(step * 4, 2)],
+                vs.at[2, step], vr.at[2, step], right,
+            ),
+            send(
+                pair(wp, n, 2), zrb.at[pl.ds(step * 4 + 2, 2)],
+                vs.at[3, step], vr.at[3, step], left,
+            ),
+        )
+
+    def last_far_out(*steps):
+        @pl.when(jnp.logical_not(owns))
+        def _():
+            for step in steps:
+                start(last_far(step))
+
+    def last_near_on(step):
+        def add(way):
+            last_far(step)[way].wait_recv()
+            n = unit(turn(y, step), near) + way
+            wp[n, rows2] = (wp[n, rows2].astype(F32) + zhb[step * 2 + way].astype(F32)).astype(BF16)
+            last_near(step)[way].start()
+
+        @pl.when(from_left)
+        def _():
+            add(1)
+
+        @pl.when(jnp.logical_not(from_left))
+        def _():
+            add(0)
+
+    def last_sum(step):
+        for copy in last_near(step):
+            copy.wait_recv()
+        for core in range(2):
+            n = unit(turn(y, step), odd) + core
+            total = wp[n, rows2].astype(F32)
+            for way in range(2):
+                total = total + zrb[step * 4 + way * 2 + core].astype(F32)
+            wp[n, rows2] = total.astype(BF16)
+
     products(turn(y, 2), zza)
-    start(halves(zza))
-    products(turn(y, 2), zzb)
-    start(halves(zzb))
+    start(halves(zza, 0))
+    start(halves(zza, 1))
+    last_far_out(2)
     products(turn(y, 1), zza)
     products(turn(y, 3), zza)
-    merge(zza)
+    last_far_out(1, 3)
+    products(turn(y, 2), zzb)
+    merge(zza, 0)
+    start(halves(zzb, 0))
+    merge(zza, 1)
+    start(halves(zzb, 1))
     products(turn(y, 1), zzb)
     products(turn(y, 3), zzb)
-    merge(zzb)
     products(y, zza)
+    last_far_out(0)
     products(y, zzb)
+    last_near_on(2)
+    last_near_on(1)
+    last_near_on(3)
+    merge(zzb, 0)
+    merge(zzb, 1)
+    last_near_on(0)
+
+    @pl.when(owns)
+    def _():
+        last_sum(2)
+        start(halves(odd, 2))
 
     def to_sibling(xx):
         return send(q.at[xx * 2 + 1 - c], qa.at[xx], qs.at[xx], qr.at[xx], sibling)
@@ -434,46 +569,87 @@
         def _():
             to_column(xx).start()
 
-    def summed(zz, core):
-        n = unit(y, zz) + core
-        return wp[n].astype(F32) + yr[0, zz, core].astype(F32) + yr[1, zz, core].astype(F32)
-
-    def wait_ways(zz):
-        for copy in ways(zz):
+    def far_z(h):
+        return (
+            send(one(base, odd * 2, h), one(zh, 0, h), zs.at[0, h], zrs.at[0, h], right),
+            send(one(base, odd * 2 + 1, h), one(zh, 1, h), zs.at[1, h], zrs.at[1, h], left),
+        )
+
+    def near_z(h):
+        return (
+            send(pair(base, near * 2, h), pair(zr, 0, h), zs.at[2, h], zrs.at[2, h], right),
+            send(pair(base, near * 2, h), pair(zr, 2, h), zs.at[3, h], zrs.at[3, h], left),
+        )
+
+    def total_y(zz, h):
+        rows = pl.ds(START[h], SIZE[h])
+        for copy in ways(zz, h):
             copy.wait_recv()
-
-    far_z = (
-        send(base.at[odd, 0], zh.at[0], zs.at[0], zrs.at[0], right),
-        send(base.at[odd, 1], zh.at[1], zs.at[1], zrs.at[1], left),
-    )
-    near_z = (
-        send(base.at[near], zr.at[0], zs.at[2], zrs.at[2], right),
-        send(base.at[near], zr.at[1], zs.at[3], zrs.at[3], left),
-    )
-
-    def total_y(zz):
-        wait_ways(zz)
         for core in range(2):
-            base[zz, core] = summed(zz, core).astype(BF16)
-
-    def near_on():
+            total = wp[unit(y, zz) + core, rows].astype(F32)
+            for way in range(2):
+                total = total + yr[way * 4 + zz * 2 + core, rows].astype(F32)
+            base[zz * 2 + core, rows] = total.astype(BF16)
+
+    def near_on(h):
+        rows = pl.ds(START[h], SIZE[h])
+
+        def add(way):
+            far_z(h)[way].wait_recv()
+            n = near * 2 + way
+            base[n, rows] = (base[n, rows].astype(F32) + zh[way, rows].astype(F32)).astype(BF16)
+            near_z(h)[way].start()
+
         @pl.when(from_left)
         def _():
-            far_z[1].wait_recv()
-            base[near, 1] = (base[near, 1].astype(F32) + zh[1].astype(F32)).astype(BF16)
-            near_z[1].start()
+            add(1)
 
         @pl.when(jnp.logical_not(from_left))
         def _():
-            far_z[0].wait_recv()
-            base[near, 0] = (base[near, 0].astype(F32) + zh[0].astype(F32)).astype(BF16)
-            near_z[0].start()
-
-    total_y(zza)
-
-    @pl.when(jnp.logical_not(owns))
-    def _():
-        start(far_z)
+            add(0)
+
+    def homeward(core, h):
+        rows = wg.at[pl.ds(START[h], SIZE[h])]
+        return send(one(final, core, h), rows, ps.at[core, h], pr.at[h], device(x, z, y, core))
+
+    def finish(h):
+        rows = pl.ds(START[h], SIZE[h])
+        if h < 2:
+            near_z(h)[0].wait_recv()
+            near_z(h)[1].wait_recv()
+        for core in range(2):
+            total = base[odd * 2 + core, rows].astype(F32)
+            for way in range(2 if h < 2 else 0):
+                total = total + zr[way * 2 + core, rows].astype(F32)
+            final[core, rows] = total.astype(BF16)
+            here = jnp.logical_and(diagonal, c == core)
+
+            @pl.when(here)
+            def _():
+                wg[rows] = final[core, rows]
+
+            @pl.when(jnp.logical_not(here))
+            def _():
+                homeward(core, h).start()
+
+    @pl.when(owns)
+    def _():
+        last_sum(1)
+        last_sum(3)
+        merge(odd, 2)
+        last_sum(0)
+
+    for h in range(2):
+        total_y(zza, h)
+
+        @pl.when(jnp.logical_not(owns))
+        def _():
+            start(far_z(h))
+
+    @pl.when(owns)
+    def _():
+        near_on(0)
+        near_on(1)
 
     rows_t = xin
 
@@ -491,12 +667,25 @@
             rows_t[i] = jnp.where(live, packed + pacc[i], 0.0).astype(BF16)
         gates_ref[0] = jnp.dot(gate_in[...], picks, preferred_element_type=F32).astype(BF16)[0:1]
 
-    rows_ref[0, 0] = (
-        contract(rows_t[0], fold[0], 0, 0) + contract(rows_t[1], fold[1], 0, 0)
+    rows_ref[...] = (
+        contract(fold[0], rows_t[0], 0, 0) + contract(fold[1], rows_t[1], 0, 0)
     ).astype(BF16)
 
-    total_y(zzb)
-    near_on()
+    @pl.when(owns)
+    def _():
+        total_y(odd, 2)
+        finish(2)
+
+    for h in range(2):
+        total_y(zzb, h)
+
+        @pl.when(owns)
+        def _():
+            finish(h)
+
+        @pl.when(jnp.logical_not(owns))
+        def _():
+            near_on(h)
 
     total = q[x * 2 + c].astype(F32)
     for step in range(1, 4):
@@ -505,67 +694,65 @@
         total = total + qb[xx].astype(F32)
     cgrad_ref[0, 0] = total.astype(BF16)
 
-    def homeward(core):
-        return send(final.at[core], wg, ps.at[core], pr.at[0], device(x, z, y, core))
+    @pl.when(jnp.logical_not(stays))
+    def _():
+        for h in range(3):
+            rows = wg.at[pl.ds(START[h], SIZE[h])]
+            send(rows, rows, ps.at[0, h], pr.at[h], holder).wait_recv()
+
+    wgrad_ref[0] = wg[pl.ds(0, SLAB)]
+
+    def left_already(copies):
+        for copy in copies:
+            copy.wait_send()
 
     @pl.when(owns)
     def _():
-        near_z[0].wait_recv()
-        near_z[1].wait_recv()
-        for core in range(2):
-            final[core] = (
-                base[odd, core].astype(F32) + zr[0, core].astype(F32) + zr[1, core].astype(F32)
-            ).astype(BF16)
-            here = jnp.logical_and(diagonal, c == core)
-
-            @pl.when(here)
-            def _():
-                wg[...] = final[core]
-
-            @pl.when(jnp.logical_not(here))
-            def _():
-                homeward(core).start()
+        for h in range(3):
+            for core in range(2):
+                @pl.when(jnp.logical_not(jnp.logical_and(diagonal, c == core)))
+                def _():
+                    homeward(core, h).wait_send()
+        for h in range(2):
+            left_already(along_z(h))
+        left_already(along_y(zz1, 0, 2) + beyond_y(zz1, 0, 2))
+        left_already(halves(odd, 2) + ways(odd, 2))
+        for step in range(4):
+            left_already(last_z(step))
+
+    @pl.when(jnp.logical_not(owns))
+    def _():
+        for h in range(2):
+            left_already(far_z(h))
+        for step in range(4):
+            left_already(last_far(step))
+
+    def one_way(onward_way, near_way):
+        for h in range(2):
+            onward(h)[onward_way].wait_send()
+            near_z(h)[near_way].wait_send()
+        for step in range(4):
+            last_onward(step)[onward_way].wait_send()
+            last_near(step)[near_way].wait_send()
+
+    @pl.when(from_left)
+    def _():
+        one_way(0, 1)
+
+    @pl.when(jnp.logical_not(from_left))
+    def _():
+        one_way(1, 0)
+
+    for h in range(2):
+        for zz, u in ((zz1, 0), (zz2, 1)):
+            left_already(along_y(zz, u, h) + beyond_y(zz, u, h) + halves(zz, h) + ways(zz, h))
 
     @pl.when(jnp.logical_not(stays))
     def _():
-        send(stage, wg, ps.at[0], pr.at[0], holder).wait_recv()
-
-    wgrad_ref[0] = wg[pl.ds(0, SLAB)]
-
-    @pl.when(owns)
-    def _():
-        for core in range(2):
-            @pl.when(jnp.logical_not(jnp.logical_and(diagonal, c == core)))
-            def _():
-                homeward(core).wait_send()
-        for copy in along_z():
-            copy.wait_send()
-
-    @pl.when(jnp.logical_not(owns))
-    def _():
-        for copy in far_z:
-            copy.wait_send()
-
-    @pl.when(from_left)
-    def _():
-        onward[0].wait_send()
-        near_z[1].wait_send()
-
-    @pl.when(jnp.logical_not(from_left))
-    def _():
-        onward[1].wait_send()
-        near_z[0].wait_send()
+        to_holder(2).wait_send()
 
     for copy in always:
         copy.wait_send()
-    for zz, u in ((zz1, 0), (zz2, 1)):
-        for copy in along_y(zz, u) + beyond_y(zz, u) + halves(zz) + ways(zz):
-            copy.wait_send()
-
-    @pl.when(jnp.logical_not(stays))
-    def _():
-        to_holder.wait_send()
-
     for step in range(4):
         to_sibling(turn(x, step)).wait_send()
         if step:
@@ -592,7 +779,7 @@
         kernel,
         name="relay",
         out_shape=(
-            jax.ShapeDtypeStruct((1, 1, LEN, COLS), BF16),
+            jax.ShapeDtypeStruct((COLS, LEN), BF16),
             jax.ShapeDtypeStruct((1, 1, LEN), BF16),
             jax.ShapeDtypeStruct((1, 1, LEN, INNER_DEV), BF16),
             jax.ShapeDtypeStruct((1, SLAB, INNER_DEV), BF16),
@@ -616,18 +803,21 @@
             block(2),
             block(16),
             block(2, 2),
-            block(2, 2, 2),
+            block(8),
             block(2),
-            block(2, 2),
-            block(2, 2),
+            block(4),
+            pltpu.VMEM((8, SIZE[2], LEN), BF16),
+            pltpu.VMEM((16, SIZE[2], LEN), BF16),
+            block(4),
             block(2),
             block(),
             pltpu.VMEM((8, LEN, INNER_DEV), BF16),
             pltpu.VMEM((4, LEN, INNER_DEV), BF16),
             pltpu.VMEM((4, LEN, INNER_DEV), BF16),
-            dma((12,)), dma((16,)), dma((3,)), dma((1,)), dma((8,)), dma((8, 2)), dma((4,)),
-            dma((7,)), dma((7,)), dma((2, 2)), dma((2, 2)), dma((2, 2)), dma((2, 2)),
-            dma((4,)), dma((4,)), dma((4,)), dma((4,)), dma((4,)), dma((4,)),
+            dma((12, 3)), dma((16, 3)), dma((3, 3)), dma((3,)), dma((8,)), dma((8, 2)), dma((4,)),
+            dma((7,)), dma((7,)), dma((2, 2, 3)), dma((2, 2, 3)), dma((2, 2, 3)), dma((2, 2, 3)),
+            dma((4, 2)), dma((4, 2)), dma((4,)), dma((4,)), dma((4,)), dma((4,)),
+            dma((3, 4)), dma((4, 4)), dma((4, 4)),
             pltpu.SemaphoreType.REGULAR,
         ],
         compiler_params=pltpu.CompilerParams(
@@ -637,7 +827,10 @@
 
 
 def per_device(byte_rows, context, weight, keep_list, counts, gate_vector):
-    return call(byte_rows, context, weight, keep_list, counts, gate_vector.reshape(1, COLS))
+    rows, gates, context_grad, weight_grad = call(
+        byte_rows[0, 0].T, context, weight, keep_list, counts, gate_vector.reshape(1, COLS)
+    )
+    return rows.T[None, None], gates, context_grad, weight_grad
 
 
 def solution(mesh):

time: 161 us -> 149 us (0.925)
  Pallas kernels: 149 us -> 140 us
  local copies, waits for them, and re-layouts: 8.06 us -> 5.7 us
    pallas_call x1, Pallas kernels: 149 us -> 140 us  [call(): pl.pallas_call(kernel, name='relay', out_shape=(jax.ShapeDtypeStruct((COL...]
    pallas_call x1 -> x0, local copies, waits for them, and re-layouts: 2.19 us -> none  [call(): pl.pallas_call(kernel, name='relay', out_shape=(jax.ShapeDtypeStruct((1,...]
where the time goes in v3:
time: 149 us; the launch traced here: 147 us
  Pallas kernels  140 us (94%)
  local copies, waits for them, and re-layouts  5.7 us (4%)
    pallas_call x1, Pallas kernels, call(): pl.pallas_call(kernel, name='relay', out_shape=(jax.ShapeDtypeStruct((COL...  140 us
    unnamed x10, local copies, waits for them, and re-layouts  4.44 us

profile of v3, /device:TPU:19, one launch (start us, length us, event | category | flops | bytes accessed | tf_op | source)
XLA Modules:
  0.0 146.7 jit_solution(2863215706279194208)
XLA Ops:
  1.3 1.3 reshape.11.g_ref
  2.5 139.7 %relay.1 = (bf16[584,512]{1,0:T(8,128)(2,1)}, bf16[1,1,512]{2,1,0:T(2,128)(2,1)}, bf16[1,1,512,512]{3,2,1,0:T(8,128)(2,1)}, bf16[1,292,512]{2,1,0:T(8,128)(2,1)}) custom-call(bf16[584,512]{1,0:T(8,128)(2,1)} %bitcast.6, bf16[1,1,512,512]{3,2,1,0:T(8,128)(2,1)} %ctx_ref.1, bf16[1,292,512]{2,1,0:T(8,128)(2,1)} %w_ref.1, s32[1,512]{1,0:T(1,128)} %keep_ref.1, ...), custom_call_target="tpu_custom_call" | custom-call | tf_op jit(solution)/shard_map/relay/pallas_call | solution.py:778
  142.2 0.0 copy-start.2
  142.2 0.0 copy-start
  142.2 2.0 %copy.15 = bf16[1,1,512,584]{2,3,1,0:T(8,128)(2,1)} copy(bf16[1,1,512,584]{2,3,1,0:T(8,128)(2,1)} %bitcast.7) | data formatting | bytes 1196032
  144.2 0.0 copy-done.2
  144.2 0.6 copy.16
  144.8 0.0 copy-done
  144.8 0.0 copy-start.1
  144.8 0.8 copy.17
  145.6 0.4 copy-done.1
  146.0 0.7 copy.18
Async XLA Ops:
  142.2 2.0 %copy-start.2 = (bf16[1,1,512]{2,1,0:T(2,128)(2,1)S(1)}, bf16[1,1,512]{2,1,0:T(2,128)(2,1)}, u32[]{:S(2)}) copy-start(bf16[1,1,512]{2,1,0:T(2,128)(2,1)} %get-tuple-element.17) | copy-start | bytes 3076
  142.2 2.6 %copy-start = (bf16[1,1,512,512]{3,2,1,0:T(8,128)(2,1)S(1)}, bf16[1,1,512,512]{3,2,1,0:T(8,128)(2,1)}, u32[]{:S(2)}) copy-start(bf16[1,1,512,512]{3,2,1,0:T(8,128)(2,1)} %get-tuple-element.18) | copy-start | bytes 1572868
  144.8 1.2 copy-start.1

commit v4 on v3

--- a/solution.py
+++ b/solution.py
@@ -365,13 +365,7 @@
 
     project(turn(y, 2), zz1)
 
-    @pl.when(s == 0)
-    def _():
-        rows_in.wait_recv()
-        for i in range(2):
-            spread[i] = contract(xin[i], picks, 1, 1).astype(BF16)
-
-    g = g_ref[...]
+    g = g_ref[...].reshape(1, COLS)
     first = g.astype(BF16)
     rest = g - first.astype(F32)
     second = rest.astype(BF16)
@@ -400,6 +394,9 @@
         for copy in stats:
             copy.start()
         rows_back.start()
+        rows_in.wait_recv()
+        for i in range(2):
+            spread[i] = contract(xin[i], picks, 1, 1).astype(BF16)
         for copy in stats:
             copy.wait()
         sums = st_in[0]
@@ -515,25 +512,25 @@
 
     products(turn(y, 2), zza)
     start(halves(zza, 0))
-    start(halves(zza, 1))
     last_far_out(2)
+    products(turn(y, 2), zzb)
+    start(halves(zzb, 0))
     products(turn(y, 1), zza)
     products(turn(y, 3), zza)
     last_far_out(1, 3)
-    products(turn(y, 2), zzb)
     merge(zza, 0)
-    start(halves(zzb, 0))
-    merge(zza, 1)
+    start(halves(zza, 1))
     start(halves(zzb, 1))
     products(turn(y, 1), zzb)
     products(turn(y, 3), zzb)
+    merge(zzb, 0)
     products(y, zza)
     last_far_out(0)
     products(y, zzb)
     last_near_on(2)
     last_near_on(1)
+    merge(zza, 1)
     last_near_on(3)
-    merge(zzb, 0)
     merge(zzb, 1)
     last_near_on(0)
 
@@ -639,17 +636,29 @@
         merge(odd, 2)
         last_sum(0)
 
-    for h in range(2):
+    def near_first(h):
         total_y(zza, h)
 
+        @pl.when(owns)
+        def _():
+            near_on(h)
+
         @pl.when(jnp.logical_not(owns))
         def _():
             start(far_z(h))
 
-    @pl.when(owns)
-    def _():
-        near_on(0)
-        near_on(1)
+    def near_last(h):
+        total_y(zzb, h)
+
+        @pl.when(owns)
+        def _():
+            finish(h)
+
+        @pl.when(jnp.logical_not(owns))
+        def _():
+            near_on(h)
+
+    near_first(0)
 
     rows_t = xin
 
@@ -671,21 +680,15 @@
         contract(fold[0], rows_t[0], 0, 0) + contract(fold[1], rows_t[1], 0, 0)
     ).astype(BF16)
 
+    near_last(0)
+    near_first(1)
+
     @pl.when(owns)
     def _():
         total_y(odd, 2)
         finish(2)
 
-    for h in range(2):
-        total_y(zzb, h)
-
-        @pl.when(owns)
-        def _():
-            finish(h)
-
-        @pl.when(jnp.logical_not(owns))
-        def _():
-            near_on(h)
+    near_last(1)
 
     total = q[x * 2 + c].astype(F32)
     for step in range(1, 4):
@@ -826,10 +829,27 @@
     )(*operands)
 
 
+def hand_on_kernel(*refs):
+    for source, target in zip(refs[:4], refs[4:]):
+        target[...] = source[...]
+
+
+def hand_on(*results):
+    vmem = pl.BlockSpec(memory_space=pltpu.VMEM)
+    return pl.pallas_call(
+        hand_on_kernel,
+        name="hand_on",
+        out_shape=tuple(jax.ShapeDtypeStruct(v.shape, v.dtype) for v in results),
+        in_specs=[vmem] * 4,
+        out_specs=(vmem,) * 4,
+    )(*results)
+
+
 def per_device(byte_rows, context, weight, keep_list, counts, gate_vector):
-    rows, gates, context_grad, weight_grad = call(
-        byte_rows[0, 0].T, context, weight, keep_list, counts, gate_vector.reshape(1, COLS)
+    results = call(
+        byte_rows[0, 0].T, context, weight, keep_list, counts, gate_vector
     )
+    rows, gates, context_grad, weight_grad = hand_on(*results)
     return rows.T[None, None], gates, context_grad, weight_grad
 
 

time: 149 us -> 146 us (0.980); the launches traced: 147 us -> 145 us
  local copies, waits for them, and re-layouts: 5.7 us -> 0 us
  Pallas kernels: 140 us -> 144 us
    unnamed x10 -> x0, local copies, waits for them, and re-layouts: 4.44 us -> none
    pallas_call x0 -> x1, Pallas kernels: none -> 2.44 us  [hand_on(): pl.pallas_call(hand_on_kernel, name='hand_on', out_shape=tuple((jax.Shape...]
    pallas_call x1, Pallas kernels: 140 us -> 142 us  [call(): pl.pallas_call(kernel, name='relay', out_shape=(jax.ShapeDtypeStruct((COL...]
where the time goes in v4:
time: 146 us; the launch traced here: 145 us
  Pallas kernels  144 us (99%)
    pallas_call x1, Pallas kernels, call(): pl.pallas_call(kernel, name='relay', out_shape=(jax.ShapeDtypeStruct((COL...  142 us

profile of v4, /device:TPU:19, one launch (start us, length us, event | category | flops | bytes accessed | tf_op | source)
XLA Modules:
  0.0 145.4 jit_solution(15892545861181426349)
XLA Ops:
  1.3 141.7 %relay.1 = (bf16[584,512]{1,0:T(8,128)(2,1)}, bf16[1,1,512]{2,1,0:T(2,128)(2,1)}, bf16[1,1,512,512]{3,2,1,0:T(8,128)(2,1)}, bf16[1,292,512]{2,1,0:T(8,128)(2,1)}) custom-call(bf16[584,512]{1,0:T(8,128)(2,1)} %bitcast.6, bf16[1,1,512,512]{3,2,1,0:T(8,128)(2,1)} %ctx_ref.1, bf16[1,292,512]{2,1,0:T(8,128)(2,1)} %w_ref.1, s32[1,512]{1,0:T(1,128)} %keep_ref.1, ...), custom_call_target="tpu_custom_call" | custom-call | tf_op jit(solution)/shard_map/relay/pallas_call | solution.py:781
  142.9 2.4 %hand_on.1 = (bf16[584,512]{1,0:T(8,128)(2,1)}, bf16[1,1,512]{2,1,0:T(2,128)(2,1)}, bf16[1,1,512,512]{3,2,1,0:T(8,128)(2,1)}, bf16[1,292,512]{2,1,0:T(8,128)(2,1)}) custom-call(bf16[584,512]{1,0:T(8,128)(2,1)} %get-tuple-element.12.refs_0_, bf16[1,1,512]{2,1,0:T(2,128)(2,1)} %get-tuple-element.13.refs_1_, ...), custom_call_target="tpu_custom_call" | custom-call | tf_op jit(solution)/shard_map/hand_on/pallas_call | solution.py:839

commit v5 on v4

--- a/solution.py
+++ b/solution.py
@@ -660,6 +660,16 @@
 
     near_first(0)
 
+    near_last(0)
+    near_first(1)
+
+    @pl.when(owns)
+    def _():
+        total_y(odd, 2)
+        finish(2)
+
+    near_last(1)
+
     rows_t = xin
 
     @pl.when(s == 0)
@@ -679,16 +689,6 @@
     rows_ref[...] = (
         contract(fold[0], rows_t[0], 0, 0) + contract(fold[1], rows_t[1], 0, 0)
     ).astype(BF16)
-
-    near_last(0)
-    near_first(1)
-
-    @pl.when(owns)
-    def _():
-        total_y(odd, 2)
-        finish(2)
-
-    near_last(1)
 
     total = q[x * 2 + c].astype(F32)
     for step in range(1, 4):

time: 146 us -> 146 us (level)
  no operation moved by 1% of the time
where the time goes in v5:
time: 146 us; the launch traced here: 145 us
  Pallas kernels  144 us (99%)
    pallas_call x1, Pallas kernels, call(): pl.pallas_call(kernel, name='relay', out_shape=(jax.ShapeDtypeStruct((COL...  142 us

profile of v5, /device:TPU:19, one launch (start us, length us, event | category | flops | bytes accessed | tf_op | source)
XLA Modules:
  0.0 145.4 jit_solution(7302700522700761963)
XLA Ops:
  1.3 141.7 %relay.1 = (bf16[584,512]{1,0:T(8,128)(2,1)}, bf16[1,1,512]{2,1,0:T(2,128)(2,1)}, bf16[1,1,512,512]{3,2,1,0:T(8,128)(2,1)}, bf16[1,292,512]{2,1,0:T(8,128)(2,1)}) custom-call(bf16[584,512]{1,0:T(8,128)(2,1)} %bitcast.6, bf16[1,1,512,512]{3,2,1,0:T(8,128)(2,1)} %ctx_ref.1, bf16[1,292,512]{2,1,0:T(8,128)(2,1)} %w_ref.1, s32[1,512]{1,0:T(1,128)} %keep_ref.1, ...), custom_call_target="tpu_custom_call" | custom-call | tf_op jit(solution)/shard_map/relay/pallas_call | solution.py:781
  142.9 2.4 %hand_on.1 = (bf16[584,512]{1,0:T(8,128)(2,1)}, bf16[1,1,512]{2,1,0:T(2,128)(2,1)}, bf16[1,1,512,512]{3,2,1,0:T(8,128)(2,1)}, bf16[1,292,512]{2,1,0:T(8,128)(2,1)}) custom-call(bf16[584,512]{1,0:T(8,128)(2,1)} %get-tuple-element.12.refs_0_, bf16[1,1,512]{2,1,0:T(2,128)(2,1)} %get-tuple-element.13.refs_1_, ...), custom_call_target="tpu_custom_call" | custom-call | tf_op jit(solution)/shard_map/hand_on/pallas_call | solution.py:839
